TPU v7x, 256 devices: a whole 4x4x8 slice. The times are simulated.
256 devices in a mesh: gx: 128 (over x, z, y_hi, core), ta: 2 (over y_lo).
Axes of the slice: x: 4, y: 4 (y_hi: 2, y_lo: 2; y = y_hi * 2 + y_lo), z: 8, core: 2. Of those that a mesh axis runs over, the one named last changes fastest.
Arguments:
- samples: bfloat16 [2048, 65536], P('gx', 'ta'), may hold values from -6 to 6
- gains: float32 [2, 2048, 1024], P(None, 'gx'), may hold values from -5 to 5
- slot_inputs: int32 [2048], replicated, may hold values from 0 to 2047, each once
- beam_order: int32 [1024], replicated, may hold values from 0 to 1023, each once
Outputs:
- intensity: float32 [2, 1024, 16384], P('ta', 'gx')
Inputs may be any that keep to these rules, and one draw needn't show every extreme that they name: `slot_inputs`: each input appears in exactly one slot. `beam_order`: each beam appears in exactly one slot.
All inputs are finite; a program needn't handle non-finite values.
Results may differ from a plain program's by a relative error of at most 0.0059.
Values may be sent and summed in bfloat16 or wider, within the bound.
No kernel may reach another device: no remote copies, remote signals or barrier semaphores. Data moves between devices by JAX's collectives and lax.ppermute only.
A program may use at most 128 MiB of HBM per device.

v0:
```python
import math

import jax
import jax.numpy as jnp
import numpy as np
from jax import lax
from jax.experimental import pallas as pl
from jax.experimental.pallas import tpu as pltpu
from jax.sharding import PartitionSpec as P

CHANNELS = 1024
FRAME = 2 * CHANNELS
HALF = CHANNELS
FEEDS = 256
CYL = 4
POLS = 2
TAPS = 4
UPCH = 16
BEAMS = 1024
INPUTS = 2048
IN_DEV = 16
F_DEV = 16
CH_DEV = 8
BLOCKS = 4
LANES = 128
VMEM_LIMIT = 48 * 1024 * 1024


def from_behind(block, axis, distance):
    devices = range(lax.axis_size(axis))
    route = [(i - distance, i) for i in devices if i - distance in devices]
    return lax.ppermute(block, axis, route)


def pfb_window():
    total = TAPS * FRAME
    places = np.arange(total, dtype=np.float64)
    centred = (places - (total - 1) * 0.5) / FRAME
    hann = 0.5 - 0.5 * np.cos(2.0 * math.pi * (places + 0.5) / total)
    window = np.sinc(centred) * hann
    window = window * np.sqrt(FRAME / np.sum(window * window))
    return window.reshape(TAPS, FRAME).astype(np.float32)


def folded_table():
    n = np.arange(HALF)
    lane = np.arange(LANES)
    out = np.zeros((BLOCKS, 2, HALF, 2 * LANES), np.float32)
    for block in range(BLOCKS):
        for parity in range(2):
            k = 256 * block + 8 * (lane // 4) + 2 * (lane % 4) + parity
            angle = 2.0 * math.pi / FRAME * (n[:, None] * k[None, :] % FRAME)
            out[block, parity, :, :LANES] = np.cos(angle) / math.sqrt(FRAME)
            out[block, parity, :, LANES:] = -np.sin(angle) / math.sqrt(FRAME)
    return out.astype(jnp.bfloat16)


def gain_select():
    lane = np.arange(LANES)
    out = np.zeros((256, 2 * LANES), np.float32)
    for parity in range(2):
        k = 8 * (lane // 4) + 2 * (lane % 4) + parity
        out[k, parity * LANES + lane] = 1.0
    return out.astype(jnp.bfloat16)


def north_table():
    index = np.arange(FEEDS)
    angle = 2.0 * math.pi / FEEDS * (index[:, None] * index[None, :] % FEEDS)
    scale = 1.0 / math.sqrt(FEEDS)
    table = np.concatenate([np.cos(angle), np.sin(angle)], 0) * scale
    return (table.astype(jnp.bfloat16).astype(np.float32) * 0.5).astype(jnp.bfloat16)


def fine_table():
    scale = 1.0 / math.sqrt(UPCH)
    out = np.zeros((2, F_DEV, 2, 4, 2, CH_DEV, UPCH), np.float32)
    j = np.arange(UPCH)
    angle = 2.0 * math.pi / UPCH * (j[:, None] * j[None, :] % UPCH)
    cosine, sine = np.cos(angle) * scale, np.sin(angle) * scale
    for parity in range(2):
        for h in range(4):
            channel = 2 * h + parity
            out[0, :, parity, h, 0, channel, :] = cosine
            out[0, :, parity, h, 1, channel, :] = -sine
            out[1, :, parity, h, 0, channel, :] = sine
            out[1, :, parity, h, 1, channel, :] = cosine
    return out.reshape(256, 256).astype(jnp.bfloat16)


def swap_groups(arrays):
    lane = lax.broadcasted_iota(jnp.int32, arrays[0].shape, 1) // 4
    arrays = list(arrays)
    for bit in (16, 8, 4, 2, 1):
        low = (lane & bit) == 0
        for j in range(32):
            if j & bit:
                continue
            a, b = arrays[j], arrays[j | bit]
            arrays[j] = jnp.where(low, a, pltpu.roll(b, 4 * bit, 1))
            arrays[j | bit] = jnp.where(low, pltpu.roll(a, LANES - 4 * bit, 1), b)
    return arrays


def channelize_kernel(x_ref, prior_ref, w_ref, t_ref, sel_ref, g_ref, out_ref, z_ref):
    block = pl.program_id(0)

    @pl.when(block == 0)
    def _():
        def chunk(c, carry):
            even_odd = []
            for half in range(2):
                at = pl.multiple_of(half * HALF + c * LANES, LANES)
                w = [w_ref[t : t + 1, pl.ds(at, LANES)] for t in range(TAPS)]
                frames = []
                for f in range(TAPS - 1):
                    frames.append(prior_ref[:, pl.ds(f * FRAME + at, LANES)].astype(jnp.float32))
                rows = []
                for f in range(F_DEV):
                    frames.append(x_ref[:, pl.ds(f * FRAME + at, LANES)].astype(jnp.float32))
                    total = frames[f] * w[0]
                    for t in range(1, TAPS):
                        total = total + frames[f + t] * w[t]
                    rows.append(total)
                even_odd.append(rows)
            to = pl.multiple_of(c * LANES, LANES)
            for f in range(F_DEV):
                a, b = even_odd[0][f], even_odd[1][f]
                rows = pl.ds(f * IN_DEV, IN_DEV)
                z_ref[0, rows, pl.ds(to, LANES)] = (a + b).astype(jnp.bfloat16)
                z_ref[1, rows, pl.ds(to, LANES)] = (a - b).astype(jnp.bfloat16)
            return carry

        lax.fori_loop(0, HALF // LANES, chunk, 0)

    g = jnp.concatenate([g_ref[0], g_ref[1]], 0)
    g_hi = g.astype(jnp.bfloat16)
    rest = g - g_hi.astype(jnp.float32)
    g_mid = rest.astype(jnp.bfloat16)
    g_low = (rest - g_mid.astype(jnp.float32)).astype(jnp.bfloat16)
    parts = jnp.concatenate([g_hi, g_mid, g_low], 0)
    picked = jnp.dot(parts, sel_ref[...], preferred_element_type=jnp.float32)
    picked = picked[0:32] + picked[32:64] + picked[64:96]
    real, imag = [], []
    for f in range(F_DEV):
        real.append([None, None])
        imag.append([None, None])
    for parity in range(2):
        spectra = jnp.dot(z_ref[parity], t_ref[0, parity], preferred_element_type=jnp.float32)
        g_re = picked[0:16, parity * LANES : (parity + 1) * LANES]
        g_im = picked[16:32, parity * LANES : (parity + 1) * LANES]
        for f in range(F_DEV):
            s_re = spectra[f * IN_DEV : (f + 1) * IN_DEV, :LANES]
            s_im = spectra[f * IN_DEV : (f + 1) * IN_DEV, LANES:]
            real[f][parity] = g_re * s_re - g_im * s_im
            imag[f][parity] = g_re * s_im + g_im * s_re
    for part, values in enumerate((real, imag)):
        arrays = swap_groups([values[j // 2][j % 2] for j in range(32)])
        for d in range(32):
            out_ref[pl.ds(d * IN_DEV, IN_DEV), pl.ds(part * LANES, LANES)] = arrays[d].astype(
                jnp.bfloat16
            )


def channelize(samples, prior, gains):
    return pl.pallas_call(
        channelize_kernel,
        grid=(BLOCKS,),
        in_specs=[
            pl.BlockSpec((IN_DEV, F_DEV * FRAME), lambda b: (0, 0)),
            pl.BlockSpec((IN_DEV, (TAPS - 1) * FRAME), lambda b: (0, 0)),
            pl.BlockSpec((TAPS, FRAME), lambda b: (0, 0)),
            pl.BlockSpec((1, 2, HALF, 2 * LANES), lambda b: (b, 0, 0, 0)),
            pl.BlockSpec((256, 256), lambda b: (0, 0)),
            pl.BlockSpec((2, IN_DEV, 256), lambda b: (0, 0, b)),
        ],
        out_specs=pl.BlockSpec((32 * IN_DEV, 256), lambda b: (b, 0)),
        out_shape=jax.ShapeDtypeStruct((INPUTS, 256), jnp.bfloat16),
        scratch_shapes=[pltpu.VMEM((2, F_DEV * IN_DEV, HALF), jnp.bfloat16)],
        compiler_params=pltpu.CompilerParams(vmem_limit_bytes=VMEM_LIMIT),
        cost_estimate=pl.CostEstimate(
            flops=2 * 256 * 1024 * 2048, bytes_accessed=7 * 1024 * 1024, transcendentals=0
        ),
        name="channelize",
    )(
        samples,
        prior,
        jnp.asarray(pfb_window()),
        jnp.asarray(folded_table()),
        jnp.asarray(gain_select()),
        gains,
    )


def beam_kernel(x_ref, pick_ref, order_ref, north_ref, fine_ref, out_ref, y_ref, beam_ref, power_ref):
    step = pl.program_id(0)
    cyl = lax.rem(step, CYL)
    fed = jnp.dot(pick_ref[...], x_ref[...], preferred_element_type=jnp.float32)
    both = jnp.dot(
        north_ref[...], fed.astype(jnp.bfloat16), preferred_element_type=jnp.float32
    )
    y_ref[cyl, 0] = both[:FEEDS, :LANES] + both[FEEDS:, LANES:]
    y_ref[cyl, 1] = both[:FEEDS, LANES:] - both[FEEDS:, :LANES]

    @pl.when(cyl == CYL - 1)
    def _():
        re = [y_ref[c, 0] for c in range(CYL)]
        im = [y_ref[c, 1] for c in range(CYL)]
        sum_re, dif_re = re[0] + re[2], re[0] - re[2]
        sum_im, dif_im = im[0] + im[2], im[0] - im[2]
        odd_re, odd_dif_re = re[1] + re[3], re[1] - re[3]
        odd_im, odd_dif_im = im[1] + im[3], im[1] - im[3]
        east = (
            (sum_re + odd_re, sum_im + odd_im),
            (dif_re + odd_dif_im, dif_im - odd_dif_re),
            (sum_re - odd_re, sum_im - odd_im),
            (dif_re - odd_dif_im, dif_im + odd_dif_re),
        )
        for e in range(CYL):
            beam_ref[pl.ds(e * FEEDS, FEEDS), :LANES] = east[e][0].astype(jnp.bfloat16)
            beam_ref[pl.ds(e * FEEDS, FEEDS), LANES:] = east[e][1].astype(jnp.bfloat16)
        fine = jnp.dot(beam_ref[...], fine_ref[...], preferred_element_type=jnp.float32)
        squares = fine * fine
        power = squares[:, :LANES] + squares[:, LANES:]

        @pl.when(step == CYL - 1)
        def _():
            power_ref[...] = power

        @pl.when(step == 2 * CYL - 1)
        def _():
            total = (0.25 * (power_ref[...] + power)).astype(jnp.bfloat16)
            out_ref[...] = jnp.dot(
                order_ref[...], total, preferred_element_type=jnp.float32
            ).astype(jnp.bfloat16)


def form_beams(piece, pick, order):
    return pl.pallas_call(
        beam_kernel,
        grid=(POLS * CYL,),
        in_specs=[
            pl.BlockSpec((INPUTS, 256), lambda s: (0, 0)),
            pl.BlockSpec((FEEDS, INPUTS), lambda s: (s, 0)),
            pl.BlockSpec((BEAMS, BEAMS), lambda s: (0, 0)),
            pl.BlockSpec((2 * FEEDS, FEEDS), lambda s: (0, 0)),
            pl.BlockSpec((256, 256), lambda s: (0, 0)),
        ],
        out_specs=pl.BlockSpec((BEAMS, LANES), lambda s: (0, 0)),
        out_shape=jax.ShapeDtypeStruct((BEAMS, LANES), jnp.bfloat16),
        scratch_shapes=[
            pltpu.VMEM((CYL, 2, FEEDS, LANES), jnp.float32),
            pltpu.VMEM((BEAMS, 256), jnp.bfloat16),
            pltpu.VMEM((BEAMS, LANES), jnp.float32),
        ],
        compiler_params=pltpu.CompilerParams(vmem_limit_bytes=VMEM_LIMIT),
        cost_estimate=pl.CostEstimate(
            flops=2 * 1024 * 1024 * 1500, bytes_accessed=12 * 1024 * 1024, transcendentals=0
        ),
        name="form_beams",
    )(piece, pick, order, jnp.asarray(north_table()), jnp.asarray(fine_table()))


def widen_kernel(x_ref, out_ref):
    for g in range(CHANNELS // CH_DEV):
        out_ref[0, :, g * LANES : (g + 1) * LANES] = x_ref[g].astype(jnp.float32)


def widen(power):
    slots = power.shape[0] * CH_DEV // CHANNELS
    return pl.pallas_call(
        widen_kernel,
        out_shape=jax.ShapeDtypeStruct((1, slots, CHANNELS * UPCH), jnp.float32),
        compiler_params=pltpu.CompilerParams(vmem_limit_bytes=VMEM_LIMIT),
        name="widen",
    )(power.reshape(CHANNELS // CH_DEV, slots, LANES))


def body(samples, gains, slot_inputs, beam_order):
    tail = samples[:, (F_DEV - TAPS + 1) * FRAME :]
    prior = from_behind(tail, "ta", 1)
    calibrated = channelize(samples, prior, gains)
    piece = lax.all_to_all(calibrated, "gx", split_axis=0, concat_axis=0, tiled=True)
    pick = (slot_inputs[:, None] == jnp.arange(INPUTS, dtype=jnp.int32)[None, :]).astype(jnp.bfloat16)
    order = (beam_order[:, None] == jnp.arange(BEAMS, dtype=jnp.int32)[None, :]).astype(jnp.bfloat16)
    power = form_beams(piece, pick, order)
    owned = lax.all_to_all(power, "gx", split_axis=0, concat_axis=0, tiled=True)
    return widen(owned)


def solution(mesh):
    placed = (P("gx", "ta"), P(None, "gx", None), P(), P())
    return jax.shard_map(
        body, mesh=mesh, in_specs=placed, out_specs=P("ta", "gx", None), check_vma=False
    )
```

profile of v0, /device:TPU:1, one launch (start us, length us, event | category | flops | bytes accessed | tf_op | source)
XLA Modules:
  0.0 99.9 jit_solution(11236294062653946844)
XLA Ops:
  0.0 0.0 copy-start.7
  0.0 0.0 copy-start.6
  0.0 1.0 slice.3
  1.0 4.0 %collective-permute-start = (bf16[16,6144]{1,0:T(8,128)(2,1)S(1)}, bf16[16,6144]{1,0:T(8,128)(2,1)S(1)}, u32[]{:S(2)}, u32[]{:S(2)}) collective-permute-start(bf16[16,6144]{1,0:T(8,128)(2,1)S(1)} %slice.3), channel_id=1, source_target_pairs={{0,1},{2,3},{4,5},{6,7},{8,9},{10,11},{12,13},{14,15},{16,17},{18,... | collective-permute-start | bytes 589832 | tf_op jit(solution)/shard_map/ppermute | solution.py:32
  5.0 3.5 %collective-permute-done.prior_ref = bf16[16,6144]{1,0:T(8,128)(2,1)S(1)} collective-permute-done((bf16[16,6144]{1,0:T(8,128)(2,1)S(1)}, bf16[16,6144]{1,0:T(8,128)(2,1)S(1)}, u32[]{:S(2)}, u32[]{:S(2)}) %collective-permute-start) | collective-permute-done | bytes 196640 | tf_op jit(solution)/shard_map/ppermute | solution.py:32
  8.6 0.0 copy-start
  8.6 1.2 %copy-done = bf16[16,32768]{1,0:T(8,128)(2,1)S(1)} copy-done((bf16[16,32768]{1,0:T(8,128)(2,1)S(1)}, bf16[16,32768]{1,0:T(8,128)(2,1)}, u32[]{:S(2)}) %copy-start) | copy-done | bytes 1048600
  9.8 0.0 copy-start.3
  9.8 0.9 copy-done.3
  10.7 0.0 copy-start.4
  10.7 0.9 copy-done.4
  11.6 0.0 copy-start.5
  11.6 0.8 copy-done.5
  12.4 6.7 %channelize.1 = bf16[2048,256]{1,0:T(8,128)(2,1)} custom-call(bf16[16,32768]{1,0:T(8,128)(2,1)S(1)} %copy-done, bf16[16,6144]{1,0:T(8,128)(2,1)S(1)} %collective-permute-done.prior_ref, f32[4,2048]{1,0:T(4,128)S(1)} %copy-done.5, bf16[4,2,1024,256]{3,2,1,0:T(8,128)(2,1)} %constant.11.clone.t_ref, bf16[256,256]{1,0:T(8,128)(2,1)S(1)} %copy-done.4, ...), custom_call_target="tpu_custom_call" | custom-call | flops 1073741824 | bytes 7340032 | tf_op jit(solution)/shard_map/channelize/pallas_call | solution.py:166
  19.0 16.2 %all-to-all-start = ((bf16[128,16,256]{2,1,0:T(8,128)(2,1)}), bf16[128,16,256]{2,1,0:T(8,128)(2,1)S(1)}, u32[]{:S(2)}, u32[]{:S(2)}) async-start(bf16[128,16,256]{2,1,0:T(8,128)(2,1)} %bitcast), calls=%async_computation | async-start | bytes 2097152 | tf_op jit(solution)/shard_map/all_to_all | solution.py:283
  35.2 0.0 copy-done.7
  35.2 0.4 fusion.1.order_ref
  35.6 0.0 copy-done.6
  35.6 0.0 copy-start.1
  35.6 0.0 copy-start.2
  35.7 4.6 %fusion.pick_ref = bf16[2048,2048]{1,0:T(8,128)(2,1)} fusion(s32[2048]{0:T(1024)S(1)} %copy-done.6), kind=kLoop, calls=%fused_computation.1 | loop fusion | flops 8388608 | bytes 8396800 | tf_op jit(solution)/shard_map/convert_element_type | solution.py:284
  40.3 24.8 %all-to-all-done = bf16[128,16,256]{2,1,0:T(8,128)(2,1)S(1)} async-done(((bf16[128,16,256]{2,1,0:T(8,128)(2,1)}), bf16[128,16,256]{2,1,0:T(8,128)(2,1)S(1)}, u32[]{:S(2)}, u32[]{:S(2)}) %all-to-all-start) | async-done | bytes 1048608 | tf_op jit(solution)/shard_map/all_to_all | solution.py:283
  65.1 0.0 copy-done.1
  65.1 0.0 copy-done.2
  65.1 10.2 %form_beams.1 = bf16[1024,128]{1,0:T(8,128)(2,1)S(1)} custom-call(bf16[2048,256]{1,0:T(8,128)(2,1)S(1)} %bitcast.3, bf16[2048,2048]{1,0:T(8,128)(2,1)} %fusion.pick_ref, bf16[1024,1024]{1,0:T(8,128)(2,1)S(1)} %fusion.1.order_ref, bf16[512,256]{1,0:T(8,128)(2,1)S(1)} %copy-done.1, bf16[256,256]{1,0:T(8,128)(2,1)S(1)} %copy-done.2), custom_call_target="tpu_custom_call" | custom-call | flops 3145728000 | bytes 12582912 | tf_op jit(solution)/shard_map/form_beams/pallas_call | solution.py:239
  75.3 23.7 %all_to_all.20.x_ref = bf16[128,8,128]{2,1,0:T(8,128)(2,1)S(1)} all-to-all(bf16[128,8,128]{2,1,0:T(8,128)(2,1)S(1)} %bitcast.4), channel_id=1, replica_groups=mesh['gx'=128,'ta'=2] {'gx'}, dimensions={0} | all-to-all | bytes 524288 | tf_op jit(solution)/shard_map/all_to_all | solution.py:287
  99.0 0.8 widen.1
Async XLA Ops:
  0.0 35.2 %copy-start.7 = (s32[1024]{0:T(1024)S(1)}, s32[1024]{0:T(1024)}, u32[]{:S(2)}) copy-start(s32[1024]{0:T(1024)} %param.12) | copy-start | bytes 12292
  0.0 35.6 %copy-start.6 = (s32[2048]{0:T(1024)S(1)}, s32[2048]{0:T(1024)}, u32[]{:S(2)}) copy-start(s32[2048]{0:T(1024)} %param.11) | copy-start | bytes 24580
  1.0 7.6 %collective-permute-start = (bf16[16,6144]{1,0:T(8,128)(2,1)S(1)}, bf16[16,6144]{1,0:T(8,128)(2,1)S(1)}, u32[]{:S(2)}, u32[]{:S(2)}) collective-permute-start(bf16[16,6144]{1,0:T(8,128)(2,1)S(1)} %slice.3), channel_id=1, source_target_pairs={{0,1},{2,3},{4,5},{6,7},{8,9},{10,11},{12,13},{14,15},{16,17},{18,... | collective-permute-start | bytes 589832 | tf_op jit(solution)/shard_map/ppermute | solution.py:32
  8.6 1.2 %copy-start = (bf16[16,32768]{1,0:T(8,128)(2,1)S(1)}, bf16[16,32768]{1,0:T(8,128)(2,1)}, u32[]{:S(2)}) copy-start(bf16[16,32768]{1,0:T(8,128)(2,1)} %x_ref.1) | copy-start | bytes 3145732
  9.8 0.9 copy-start.3
  10.7 0.9 copy-start.4
  11.6 0.8 copy-start.5
  19.0 46.1 %all-to-all-start = ((bf16[128,16,256]{2,1,0:T(8,128)(2,1)}), bf16[128,16,256]{2,1,0:T(8,128)(2,1)S(1)}, u32[]{:S(2)}, u32[]{:S(2)}) async-start(bf16[128,16,256]{2,1,0:T(8,128)(2,1)} %bitcast), calls=%async_computation | async-start | bytes 2097152 | tf_op jit(solution)/shard_map/all_to_all | solution.py:283
  35.6 29.5 %copy-start.1 = (bf16[512,256]{1,0:T(8,128)(2,1)S(1)}, bf16[512,256]{1,0:T(8,128)(2,1)}, u32[]{:S(2)}) copy-start(bf16[512,256]{1,0:T(8,128)(2,1)} %constant.13.clone.north_ref) | copy-start | bytes 786436
  35.6 29.5 %copy-start.2 = (bf16[256,256]{1,0:T(8,128)(2,1)S(1)}, bf16[256,256]{1,0:T(8,128)(2,1)}, u32[]{:S(2)}) copy-start(bf16[256,256]{1,0:T(8,128)(2,1)} %constant.14.clone.fine_ref) | copy-start | bytes 393220
where the time goes:
time: 100 us; the launch traced here: 99.9 us
  waiting for transfers between devices  28.3 us (28%)
  blocking collectives  23.7 us (24%)
  starting transfers between devices  20.2 us (20%)
  Pallas kernels  17.7 us (18%)
  other arithmetic  5.04 us (5%)
  local copies, waits for them, and re-layouts  4.78 us (5%)
    all_to_all x1, waiting for transfers between devices, body(): lax.all_to_all(calibrated, 'gx', split_axis=0, concat_axis=0, tiled=True)  24.8 us
    all_to_all x1, blocking collectives, body(): owned = lax.all_to_all(power, 'gx', split_axis=0, concat_axis=0, tiled=True)  23.7 us
    all_to_all x1, starting transfers between devices, body(): lax.all_to_all(calibrated, 'gx', split_axis=0, concat_axis=0, tiled=True)  16.2 us
    pallas_call x1, Pallas kernels, form_beams(): pl.pallas_call(beam_kernel, grid=(POLS * CYL,), in_specs=[pl.BlockSpec((I...  10.2 us
    pallas_call x1, Pallas kernels, channelize(): pl.pallas_call(channelize_kernel, grid=(BLOCKS,), in_specs=[pl.BlockSpec(...  6.67 us
    convert_element_type x1, other arithmetic, body(): (slot_inputs[:, None] == jnp.arange(INPUTS, dtype=jnp.int32)[None, :]).as...  4.64 us
    ppermute x1, starting transfers between devices, from_behind(): return lax.ppermute(block, axis, route)  4.04 us
    unnamed x16, local copies, waits for them, and re-layouts  3.81 us
  transfers between devices with their start and end apart: 2, of which 2 were waited for; matrix products, arithmetic and copies ran while one was open for 5% of the time, Pallas kernels for 0%

commit v1 on v0

v1 whole, which is shorter than its diff:
```python
import math

import jax
import jax.numpy as jnp
import numpy as np
from jax import lax
from jax.experimental import pallas as pl
from jax.experimental.pallas import tpu as pltpu
from jax.sharding import PartitionSpec as P

CHANNELS = 1024
FRAME = 2 * CHANNELS
HALF = CHANNELS
FEEDS = 256
CYL = 4
POLS = 2
TAPS = 4
UPCH = 16
BEAMS = 1024
INPUTS = 2048
IN_DEV = 16
F_DEV = 16
CH_DEV = 8
BLOCKS = 4
LANES = 128
LATER = F_DEV - TAPS + 1
ALL_VMEM = 40 * 1024 * 1024
BEAM_VMEM = 32 * 1024 * 1024


def from_behind(block, axis, distance):
    devices = range(lax.axis_size(axis))
    route = [(i - distance, i) for i in devices if i - distance in devices]
    return lax.ppermute(block, axis, route)


def pfb_window():
    total = TAPS * FRAME
    places = np.arange(total, dtype=np.float64)
    centred = (places - (total - 1) * 0.5) / FRAME
    hann = 0.5 - 0.5 * np.cos(2.0 * math.pi * (places + 0.5) / total)
    window = np.sinc(centred) * hann
    window = window * np.sqrt(FRAME / np.sum(window * window))
    return window.reshape(TAPS, FRAME).astype(np.float32)


def folded_table():
    n = np.arange(HALF)
    lane = np.arange(LANES)
    out = np.zeros((BLOCKS, 2, HALF, 2 * LANES), np.float32)
    for block in range(BLOCKS):
        for parity in range(2):
            k = 256 * block + 8 * (lane // 4) + 2 * (lane % 4) + parity
            angle = 2.0 * math.pi / FRAME * (n[:, None] * k[None, :] % FRAME)
            out[block, parity, :, :LANES] = np.cos(angle) / math.sqrt(FRAME)
            out[block, parity, :, LANES:] = -np.sin(angle) / math.sqrt(FRAME)
    return out.astype(jnp.bfloat16)


def gain_select():
    lane = np.arange(LANES)
    out = np.zeros((256, 2 * LANES), np.float32)
    for parity in range(2):
        k = 8 * (lane // 4) + 2 * (lane % 4) + parity
        out[k, parity * LANES + lane] = 1.0
    return out.astype(jnp.bfloat16)


def north_table():
    index = np.arange(FEEDS)
    angle = 2.0 * math.pi / FEEDS * (index[:, None] * index[None, :] % FEEDS)
    scale = 1.0 / math.sqrt(FEEDS)
    table = np.concatenate([np.cos(angle), np.sin(angle)], 0) * scale
    return (table.astype(jnp.bfloat16).astype(np.float32) * 0.5).astype(jnp.bfloat16)


def fine_table():
    scale = 1.0 / math.sqrt(UPCH)
    out = np.zeros((2, F_DEV, 2, 4, 2, CH_DEV, UPCH), np.float32)
    j = np.arange(UPCH)
    angle = 2.0 * math.pi / UPCH * (j[:, None] * j[None, :] % UPCH)
    cosine, sine = np.cos(angle) * scale, np.sin(angle) * scale
    for parity in range(2):
        for h in range(4):
            channel = 2 * h + parity
            out[0, :, parity, h, 0, channel, :] = cosine
            out[0, :, parity, h, 1, channel, :] = -sine
            out[1, :, parity, h, 0, channel, :] = sine
            out[1, :, parity, h, 1, channel, :] = cosine
    return out.reshape(256, 256).astype(jnp.bfloat16)


def swap_groups(arrays):
    lane = lax.broadcasted_iota(jnp.int32, arrays[0].shape, 1) // 4
    arrays = list(arrays)
    for bit in (16, 8, 4, 2, 1):
        low = (lane & bit) == 0
        for j in range(32):
            if j & bit:
                continue
            a, b = arrays[j], arrays[j | bit]
            arrays[j] = jnp.where(low, a, pltpu.roll(b, 4 * bit, 1))
            arrays[j | bit] = jnp.where(low, pltpu.roll(a, LANES - 4 * bit, 1), b)
    return arrays


def filter_frames(frames, w, first, count):
    rows = []
    for f in range(first, first + count):
        total = frames[f - TAPS + 1] * w[0]
        for t in range(1, TAPS):
            total = total + frames[f - TAPS + 1 + t] * w[t]
        rows.append(total)
    return rows


def fold_frames(parts, w_ref, z_ref, count):
    def chunk(c, carry):
        halves = []
        for half in range(2):
            at = pl.multiple_of(half * HALF + c * LANES, LANES)
            w = [w_ref[t : t + 1, pl.ds(at, LANES)] for t in range(TAPS)]
            frames = []
            for ref in parts:
                for f in range(ref.shape[1] // FRAME):
                    frames.append(ref[:, pl.ds(f * FRAME + at, LANES)].astype(jnp.float32))
            halves.append(filter_frames(frames, w, TAPS - 1, count))
        to = pl.ds(pl.multiple_of(c * LANES, LANES), LANES)
        for f in range(count):
            a, b = halves[0][f], halves[1][f]
            z_ref[0, pl.ds(f * IN_DEV, IN_DEV), to] = (a + b).astype(jnp.bfloat16)
            z_ref[1, pl.ds(f * IN_DEV, IN_DEV), to] = (a - b).astype(jnp.bfloat16)
        return carry

    lax.fori_loop(0, HALF // LANES, chunk, 0)


def calibrate(z, table, gain_re, gain_im):
    spectra = jnp.dot(z, table, preferred_element_type=jnp.float32)
    real, imag = [], []
    for f in range(z.shape[0] // IN_DEV):
        s_re = spectra[f * IN_DEV : (f + 1) * IN_DEV, :LANES]
        s_im = spectra[f * IN_DEV : (f + 1) * IN_DEV, LANES:]
        real.append(gain_re * s_re - gain_im * s_im)
        imag.append(gain_re * s_im + gain_im * s_re)
    return real, imag


def later_kernel(
    x_hbm, w_hbm, t_hbm, sel_hbm, g_hbm, x_ref, w_ref, t_ref, out_ref, picked_ref, sel_ref, g_ref, z_ref, sems
):
    copies = [
        pltpu.make_async_copy(x_hbm, x_ref, sems.at[0]),
        pltpu.make_async_copy(w_hbm, w_ref, sems.at[1]),
        pltpu.make_async_copy(sel_hbm, sel_ref, sems.at[2]),
        pltpu.make_async_copy(g_hbm, g_ref, sems.at[3]),
    ]
    for block in range(BLOCKS):
        copies.append(pltpu.make_async_copy(t_hbm.at[block], t_ref.at[block], sems.at[4 + block]))
    for copy in copies:
        copy.start()
    for copy in copies[:2]:
        copy.wait()
    fold_frames([x_ref], w_ref, z_ref, LATER)
    for copy in copies[2:4]:
        copy.wait()
    for block in range(BLOCKS):
        columns = slice(block * 256, (block + 1) * 256)
        g = jnp.concatenate([g_ref[0, :, columns], g_ref[1, :, columns]], 0)
        g_hi = g.astype(jnp.bfloat16)
        rest = g - g_hi.astype(jnp.float32)
        g_mid = rest.astype(jnp.bfloat16)
        g_low = (rest - g_mid.astype(jnp.float32)).astype(jnp.bfloat16)
        parts = jnp.concatenate([g_hi, g_mid, g_low], 0)
        picked = jnp.dot(parts, sel_ref[...], preferred_element_type=jnp.float32)
        picked_ref[block] = picked[0:32] + picked[32:64] + picked[64:96]
    for block in range(BLOCKS):
        copies[4 + block].wait()
        picked = picked_ref[block]
        for parity in range(2):
            lanes = slice(parity * LANES, (parity + 1) * LANES)
            real, imag = calibrate(
                z_ref[parity], t_ref[block, parity], picked[0:16, lanes], picked[16:32, lanes]
            )
            for f in range(LATER):
                rows = pl.ds(f * IN_DEV, IN_DEV)
                out_ref[block, 0, parity, rows, :] = real[f].astype(jnp.bfloat16)
                out_ref[block, 1, parity, rows, :] = imag[f].astype(jnp.bfloat16)


def first_kernel(x_ref, prior_ref, w_ref, t_ref, picked_ref, later_ref, out_hbm, z_ref, out_ref, sems):
    fold_frames([prior_ref, x_ref.at[:, : (TAPS - 1) * FRAME]], w_ref, z_ref, TAPS - 1)
    copies = []
    for block in range(BLOCKS):
        picked = picked_ref[block]
        values = [[None] * 32, [None] * 32]
        for parity in range(2):
            lanes = slice(parity * LANES, (parity + 1) * LANES)
            early = calibrate(
                z_ref[parity], t_ref[block, parity], picked[0:16, lanes], picked[16:32, lanes]
            )
            for part in range(2):
                for f in range(TAPS - 1):
                    values[part][2 * f + parity] = early[part][f].astype(jnp.bfloat16)
                for f in range(LATER):
                    rows = pl.ds(f * IN_DEV, IN_DEV)
                    values[part][2 * (f + TAPS - 1) + parity] = later_ref[block, part, parity, rows, :]
        for part in range(2):
            arrays = swap_groups(values[part])
            for d in range(32):
                rows = pl.ds((block * 32 + d) * IN_DEV, IN_DEV)
                out_ref[rows, pl.ds(part * LANES, LANES)] = arrays[d]
        rows = pl.ds(block * 32 * IN_DEV, 32 * IN_DEV)
        copies.append(pltpu.make_async_copy(out_ref.at[rows], out_hbm.at[rows], sems.at[block]))
        copies[block].start()
    for copy in copies:
        copy.wait()


IN_VMEM = pl.BlockSpec(memory_space=pltpu.VMEM)
IN_HBM = pl.BlockSpec(memory_space=pltpu.HBM)


def channelize_later(samples, gains):
    table = folded_table()
    return pl.pallas_call(
        later_kernel,
        in_specs=[IN_HBM] * 5,
        out_specs=[IN_VMEM] * 5,
        out_shape=[
            pltpu.VMEM((IN_DEV, F_DEV * FRAME), jnp.bfloat16),
            pltpu.VMEM((TAPS, FRAME), jnp.float32),
            pltpu.VMEM(table.shape, jnp.bfloat16),
            pltpu.VMEM((BLOCKS, 2, 2, LATER * IN_DEV, LANES), jnp.bfloat16),
            pltpu.VMEM((BLOCKS, 2 * IN_DEV, 2 * LANES), jnp.float32),
        ],
        scratch_shapes=[
            pltpu.VMEM((256, 256), jnp.bfloat16),
            pltpu.VMEM((2, IN_DEV, CHANNELS), jnp.float32),
            pltpu.VMEM((2, LATER * IN_DEV, HALF), jnp.bfloat16),
            pltpu.SemaphoreType.DMA((4 + BLOCKS,)),
        ],
        compiler_params=pltpu.CompilerParams(vmem_limit_bytes=ALL_VMEM),
        cost_estimate=pl.CostEstimate(
            flops=2 * 256 * 1024 * 2048, bytes_accessed=7 * 1024 * 1024, transcendentals=0
        ),
        name="channelize_later",
    )(
        *(
            pltpu.with_memory_space_constraint(x, pltpu.HBM)
            for x in (
                samples,
                jnp.asarray(pfb_window()),
                jnp.asarray(table),
                jnp.asarray(gain_select()),
                gains,
            )
        )
    )


def channelize_first(samples, prior, window, table, picked, later):
    return pl.pallas_call(
        first_kernel,
        in_specs=[IN_VMEM] * 6,
        out_specs=IN_HBM,
        out_shape=jax.ShapeDtypeStruct((INPUTS, 256), jnp.bfloat16),
        scratch_shapes=[
            pltpu.VMEM((2, (TAPS - 1) * IN_DEV, HALF), jnp.bfloat16),
            pltpu.VMEM((INPUTS, 256), jnp.bfloat16),
            pltpu.SemaphoreType.DMA((BLOCKS,)),
        ],
        compiler_params=pltpu.CompilerParams(vmem_limit_bytes=BEAM_VMEM),
        cost_estimate=pl.CostEstimate(
            flops=2 * 48 * 1024 * 2048, bytes_accessed=7 * 1024 * 1024, transcendentals=0
        ),
        name="channelize_first",
    )(samples, prior, window, table, picked, later)


def beam_kernel(x_ref, pick_ref, order_ref, north_ref, fine_ref, out_ref, fed_ref, beam_ref, power_ref):
    for pol in range(POLS):
        for cyl in range(CYL):
            rows = pl.ds((pol * CYL + cyl) * FEEDS, FEEDS)
            fed_ref[rows, :] = jnp.dot(
                pick_ref[rows, :], x_ref[...], preferred_element_type=jnp.float32
            ).astype(jnp.bfloat16)
        re, im = [], []
        for cyl in range(CYL):
            rows = pl.ds((pol * CYL + cyl) * FEEDS, FEEDS)
            both = jnp.dot(north_ref[...], fed_ref[rows, :], preferred_element_type=jnp.float32)
            re.append(both[:FEEDS, :LANES] + both[FEEDS:, LANES:])
            im.append(both[:FEEDS, LANES:] - both[FEEDS:, :LANES])
        sum_re, dif_re = re[0] + re[2], re[0] - re[2]
        sum_im, dif_im = im[0] + im[2], im[0] - im[2]
        odd_re, odd_dif_re = re[1] + re[3], re[1] - re[3]
        odd_im, odd_dif_im = im[1] + im[3], im[1] - im[3]
        east = (
            (sum_re + odd_re, sum_im + odd_im),
            (dif_re + odd_dif_im, dif_im - odd_dif_re),
            (sum_re - odd_re, sum_im - odd_im),
            (dif_re - odd_dif_im, dif_im + odd_dif_re),
        )
        for e in range(CYL):
            beam_ref[pl.ds(e * FEEDS, FEEDS), :LANES] = east[e][0].astype(jnp.bfloat16)
            beam_ref[pl.ds(e * FEEDS, FEEDS), LANES:] = east[e][1].astype(jnp.bfloat16)
        fine = jnp.dot(beam_ref[...], fine_ref[...], preferred_element_type=jnp.float32)
        squares = fine * fine
        power = squares[:, :LANES] + squares[:, LANES:]
        if pol == 0:
            power_ref[...] = power
        else:
            total = (0.25 * (power_ref[...] + power)).astype(jnp.bfloat16)
            out_ref[...] = jnp.dot(
                order_ref[...], total, preferred_element_type=jnp.float32
            ).astype(jnp.bfloat16)


def form_beams(piece, pick, order):
    return pl.pallas_call(
        beam_kernel,
        in_specs=[pl.BlockSpec(memory_space=pltpu.VMEM)] * 5,
        out_specs=pl.BlockSpec(memory_space=pltpu.VMEM),
        out_shape=jax.ShapeDtypeStruct((BEAMS, LANES), jnp.bfloat16),
        scratch_shapes=[
            pltpu.VMEM((INPUTS, 256), jnp.bfloat16),
            pltpu.VMEM((BEAMS, 256), jnp.bfloat16),
            pltpu.VMEM((BEAMS, LANES), jnp.float32),
        ],
        compiler_params=pltpu.CompilerParams(vmem_limit_bytes=BEAM_VMEM),
        cost_estimate=pl.CostEstimate(
            flops=2 * 1024 * 1024 * 1500, bytes_accessed=12 * 1024 * 1024, transcendentals=0
        ),
        name="form_beams",
    )(piece, pick, order, jnp.asarray(north_table()), jnp.asarray(fine_table()))


def widen_kernel(x_ref, out_ref):
    for g in range(CHANNELS // CH_DEV):
        out_ref[0, :, g * LANES : (g + 1) * LANES] = x_ref[g].astype(jnp.float32)


def widen(power):
    slots = power.shape[0] * CH_DEV // CHANNELS
    return pl.pallas_call(
        widen_kernel,
        out_shape=jax.ShapeDtypeStruct((1, slots, CHANNELS * UPCH), jnp.float32),
        compiler_params=pltpu.CompilerParams(vmem_limit_bytes=BEAM_VMEM),
        name="widen",
    )(power.reshape(CHANNELS // CH_DEV, slots, LANES))


def body(samples, gains, slot_inputs, beam_order):
    tail = samples[:, (F_DEV - TAPS + 1) * FRAME :]
    prior = from_behind(tail, "ta", 1)
    held, window, table, later, picked = channelize_later(samples, gains)
    calibrated = channelize_first(held, prior, window, table, picked, later)
    piece = lax.all_to_all(calibrated, "gx", split_axis=0, concat_axis=0, tiled=True)
    pick = (slot_inputs[:, None] == jnp.arange(INPUTS, dtype=jnp.int32)[None, :]).astype(jnp.bfloat16)
    order = (beam_order[:, None] == jnp.arange(BEAMS, dtype=jnp.int32)[None, :]).astype(jnp.bfloat16)
    power = form_beams(piece, pick, order)
    owned = lax.all_to_all(power, "gx", split_axis=0, concat_axis=0, tiled=True)
    return widen(owned)


def solution(mesh):
    placed = (P("gx", "ta"), P(None, "gx", None), P(), P())
    return jax.shard_map(
        body, mesh=mesh, in_specs=placed, out_specs=P("ta", "gx", None), check_vma=False
    )
```

time: 100 us -> 91.1 us (0.911)
  Pallas kernels: 17.7 us -> 12.9 us
  waiting for transfers between devices: 28.3 us -> 24.8 us
    pallas_call x2 -> x3, Pallas kernels: 16.9 us -> 12 us  [the longest x1 4.59 us: form_beams(): pl.pallas_call(beam_kernel, in_specs=[pl.BlockSpec(memory_space=pltpu.VME...]
    ppermute x1, waiting for transfers between devices: 3.54 us -> 0.01 us  [from_behind(): return lax.ppermute(block, axis, route)]
    unnamed x16 -> x10, local copies, waits for them, and re-layouts: 3.81 us -> 3.41 us
  transfers between devices with their start and end apart: 2 -> 2, of which waited for: 2 -> 1; matrix products, arithmetic and copies ran while one was open for 5% -> 6% of each run, Pallas kernels for 0% -> 4%
where the time goes in v1:
time: 91.1 us; the launch traced here: 90.8 us
  waiting for transfers between devices  24.8 us (27%)
  blocking collectives  23.7 us (26%)
  starting transfers between devices  19.9 us (22%)
  Pallas kernels  12.9 us (14%)
  other arithmetic  5.05 us (6%)
  local copies, waits for them, and re-layouts  4.35 us (5%)
    all_to_all x1, waiting for transfers between devices, body(): lax.all_to_all(calibrated, 'gx', split_axis=0, concat_axis=0, tiled=True)  24.8 us
    all_to_all x1, blocking collectives, body(): owned = lax.all_to_all(power, 'gx', split_axis=0, concat_axis=0, tiled=True)  23.7 us
    all_to_all x1, starting transfers between devices, body(): lax.all_to_all(calibrated, 'gx', split_axis=0, concat_axis=0, tiled=True)  15.9 us
    convert_element_type x1, other arithmetic, body(): (slot_inputs[:, None] == jnp.arange(INPUTS, dtype=jnp.int32)[None, :]).as...  4.65 us
    pallas_call x1, Pallas kernels, form_beams(): pl.pallas_call(beam_kernel, in_specs=[pl.BlockSpec(memory_space=pltpu.VME...  4.59 us
    ppermute x1, starting transfers between devices, from_behind(): return lax.ppermute(block, axis, route)  4.04 us
    pallas_call x1, Pallas kernels, channelize_later(): pl.pallas_call(later_kernel, in_specs=[IN_HBM] * 5, out_specs=[IN_VMEM] *...  3.77 us
    pallas_call x1, Pallas kernels, channelize_first(): pl.pallas_call(first_kernel, in_specs=[IN_VMEM] * 6, out_specs=IN_HBM, ou...  3.68 us
  transfers between devices with their start and end apart: 2, of which 1 were waited for; matrix products, arithmetic and copies ran while one was open for 6% of the time, Pallas kernels for 4%

profile of v1, /device:TPU:1, one launch (start us, length us, event | category | flops | bytes accessed | tf_op | source)
XLA Modules:
  0.0 90.8 jit_solution(3167458143960143071)
XLA Ops:
  0.0 0.9 %slice.3 = bf16[16,6144]{1,0:T(8,128)(2,1)S(1)} slice(bf16[16,32768]{1,0:T(8,128)(2,1)} %x_hbm.1), slice={[0:16], [26624:32768]} | slice | bytes 393216 | tf_op jit(solution)/shard_map/slice | solution.py:354
  0.9 4.0 %collective-permute-start = (bf16[16,6144]{1,0:T(8,128)(2,1)S(1)}, bf16[16,6144]{1,0:T(8,128)(2,1)S(1)}, u32[]{:S(2)}, u32[]{:S(2)}) collective-permute-start(bf16[16,6144]{1,0:T(8,128)(2,1)S(1)} %slice.3), channel_id=1, source_target_pairs={{0,1},{2,3},{4,5},{6,7},{8,9},{10,11},{12,13},{14,15},{16,17},{18,... | collective-permute-start | bytes 589832 | tf_op jit(solution)/shard_map/ppermute | solution.py:34
  5.0 3.8 %channelize_later.1 = (bf16[16,32768]{1,0:T(8,128)(2,1)S(1)}, f32[4,2048]{1,0:T(4,128)S(1)}, bf16[4,2,1024,256]{3,2,1,0:T(8,128)(2,1)S(1)}, bf16[4,2,2,208,128]{4,3,2,1,0:T(8,128)(2,1)S(1)}, f32[4,32,256]{2,1,0:T(8,128)S(1)}) custom-call(bf16[16,32768]{1,0:T(8,128)(2,1)} %x_hbm.1, f32[4,2048]{1,0:T(4,128)} %constant.10.clone.w_hbm, ...), custom_call_target="tpu_custom_call" | custom-call | flops 1073741824 | bytes 7340032 | tf_op jit(solution)/shard_map/channelize_later/pallas_call | solution.py:226
  8.8 0.0 collective-permute-done.prior_ref
  8.8 0.0 copy-start.4
  8.8 0.0 copy-start.3
  8.8 3.7 %channelize_first.1 = bf16[2048,256]{1,0:T(8,128)(2,1)} custom-call(bf16[16,32768]{1,0:T(8,128)(2,1)S(1)} %get-tuple-element.10.x_ref, bf16[16,6144]{1,0:T(8,128)(2,1)S(1)} %collective-permute-done.prior_ref, f32[4,2048]{1,0:T(4,128)S(1)} %get-tuple-element.11.w_ref, bf16[4,2,1024,256]{3,2,1,0:T(8,128)(2,1)S(1)} %get-tuple-element.12.t_ref, ...), custom_call_target="tpu_custom_call" | custom-call | flops 201326592 | bytes 7340032 | tf_op jit(solution)/shard_map/channelize_first/pallas_call | solution.py:263
  12.5 15.9 %all-to-all-start = ((bf16[128,16,256]{2,1,0:T(8,128)(2,1)}), bf16[128,16,256]{2,1,0:T(8,128)(2,1)S(1)}, u32[]{:S(2)}, u32[]{:S(2)}) async-start(bf16[128,16,256]{2,1,0:T(8,128)(2,1)} %bitcast), calls=%async_computation | async-start | bytes 2097152 | tf_op jit(solution)/shard_map/all_to_all | solution.py:358
  28.4 0.0 copy-done.4
  28.4 0.4 fusion.1.order_ref
  28.8 0.0 copy-done.3
  28.8 0.0 copy-start.1
  28.8 0.0 copy-start.2
  28.8 4.7 %fusion.pick_ref = bf16[2048,2048]{1,0:T(8,128)(2,1)} fusion(s32[2048]{0:T(1024)S(1)} %copy-done.3), kind=kLoop, calls=%fused_computation.1 | loop fusion | flops 8388608 | bytes 8396800 | tf_op jit(solution)/shard_map/convert_element_type | solution.py:359
  33.5 24.8 %all-to-all-done = bf16[128,16,256]{2,1,0:T(8,128)(2,1)S(1)} async-done(((bf16[128,16,256]{2,1,0:T(8,128)(2,1)}), bf16[128,16,256]{2,1,0:T(8,128)(2,1)S(1)}, u32[]{:S(2)}, u32[]{:S(2)}) %all-to-all-start) | async-done | bytes 1048608 | tf_op jit(solution)/shard_map/all_to_all | solution.py:358
  58.3 0.0 copy-done.1
  58.3 0.0 copy-done.2
  58.3 0.0 copy-start
  58.3 3.4 %copy-done = bf16[2048,2048]{1,0:T(8,128)(2,1)S(1)} copy-done((bf16[2048,2048]{1,0:T(8,128)(2,1)S(1)}, bf16[2048,2048]{1,0:T(8,128)(2,1)}, u32[]{:S(2)}) %copy-start) | copy-done | bytes 8388632
  61.7 4.6 %form_beams.1 = bf16[1024,128]{1,0:T(8,128)(2,1)S(1)} custom-call(bf16[2048,256]{1,0:T(8,128)(2,1)S(1)} %bitcast.3, bf16[2048,2048]{1,0:T(8,128)(2,1)S(1)} %copy-done, bf16[1024,1024]{1,0:T(8,128)(2,1)S(1)} %fusion.1.order_ref, bf16[512,256]{1,0:T(8,128)(2,1)S(1)} %copy-done.1, bf16[256,256]{1,0:T(8,128)(2,1)S(1)} %copy-done.2), custom_call_target="tpu_custom_call" | custom-call | flops 3145728000 | bytes 12582912 | tf_op jit(solution)/shard_map/form_beams/pallas_call | solution.py:320
  66.3 23.7 %all_to_all.20.x_ref = bf16[128,8,128]{2,1,0:T(8,128)(2,1)S(1)} all-to-all(bf16[128,8,128]{2,1,0:T(8,128)(2,1)S(1)} %bitcast.4), channel_id=1, replica_groups=mesh['gx'=128,'ta'=2] {'gx'}, dimensions={0} | all-to-all | bytes 524288 | tf_op jit(solution)/shard_map/all_to_all | solution.py:362
  90.0 0.8 widen.1
Async XLA Ops:
  0.9 7.8 %collective-permute-start = (bf16[16,6144]{1,0:T(8,128)(2,1)S(1)}, bf16[16,6144]{1,0:T(8,128)(2,1)S(1)}, u32[]{:S(2)}, u32[]{:S(2)}) collective-permute-start(bf16[16,6144]{1,0:T(8,128)(2,1)S(1)} %slice.3), channel_id=1, source_target_pairs={{0,1},{2,3},{4,5},{6,7},{8,9},{10,11},{12,13},{14,15},{16,17},{18,... | collective-permute-start | bytes 589832 | tf_op jit(solution)/shard_map/ppermute | solution.py:34
  8.8 19.6 %copy-start.4 = (s32[1024]{0:T(1024)S(1)}, s32[1024]{0:T(1024)}, u32[]{:S(2)}) copy-start(s32[1024]{0:T(1024)} %param.12) | copy-start | bytes 12292
  8.8 20.0 %copy-start.3 = (s32[2048]{0:T(1024)S(1)}, s32[2048]{0:T(1024)}, u32[]{:S(2)}) copy-start(s32[2048]{0:T(1024)} %param.11) | copy-start | bytes 24580
  12.5 45.8 %all-to-all-start = ((bf16[128,16,256]{2,1,0:T(8,128)(2,1)}), bf16[128,16,256]{2,1,0:T(8,128)(2,1)S(1)}, u32[]{:S(2)}, u32[]{:S(2)}) async-start(bf16[128,16,256]{2,1,0:T(8,128)(2,1)} %bitcast), calls=%async_computation | async-start | bytes 2097152 | tf_op jit(solution)/shard_map/all_to_all | solution.py:358
  28.8 29.5 %copy-start.1 = (bf16[512,256]{1,0:T(8,128)(2,1)S(1)}, bf16[512,256]{1,0:T(8,128)(2,1)}, u32[]{:S(2)}) copy-start(bf16[512,256]{1,0:T(8,128)(2,1)} %constant.13.clone.north_ref) | copy-start | bytes 786436
  28.8 29.5 %copy-start.2 = (bf16[256,256]{1,0:T(8,128)(2,1)S(1)}, bf16[256,256]{1,0:T(8,128)(2,1)}, u32[]{:S(2)}) copy-start(bf16[256,256]{1,0:T(8,128)(2,1)} %constant.14.clone.fine_ref) | copy-start | bytes 393220
  58.3 3.4 %copy-start = (bf16[2048,2048]{1,0:T(8,128)(2,1)S(1)}, bf16[2048,2048]{1,0:T(8,128)(2,1)}, u32[]{:S(2)}) copy-start(bf16[2048,2048]{1,0:T(8,128)(2,1)} %fusion.pick_ref) | copy-start | bytes 25165828

commit v2 on v1

--- a/solution.py
+++ b/solution.py
@@ -26,12 +26,21 @@
 LATER = F_DEV - TAPS + 1
 ALL_VMEM = 40 * 1024 * 1024
 BEAM_VMEM = 32 * 1024 * 1024
+HEAD = 256
+MADE = 1024
+RING = np.random.RandomState(3).permutation(128).tolist()
 
 
 def from_behind(block, axis, distance):
     devices = range(lax.axis_size(axis))
     route = [(i - distance, i) for i in devices if i - distance in devices]
     return lax.ppermute(block, axis, route)
+
+
+def exchange(block):
+    return lax.all_to_all(
+        block, "gx", split_axis=0, concat_axis=0, axis_index_groups=[RING], tiled=True
+    )
 
 
 def pfb_window():
@@ -278,12 +287,105 @@
     )(samples, prior, window, table, picked, later)
 
 
-def beam_kernel(x_ref, pick_ref, order_ref, north_ref, fine_ref, out_ref, fed_ref, beam_ref, power_ref):
+def one_hot_kernel(slots_ref, order_ref, ids_ref, head_ref, rest_hbm, turn_hbm, rest_ref, turn_ref, sems):
+    slots = jnp.transpose(slots_ref[...])
+    copies = []
+    for block in [*range(HEAD // LANES), *range(MADE // LANES, INPUTS // LANES)]:
+        hot = jnp.where(slots[:, block : block + 1] == ids_ref[...], 1.0, 0.0).astype(jnp.bfloat16)
+        at = block * LANES
+        if at < HEAD:
+            head_ref[pl.ds(at, LANES), :] = hot
+            continue
+        rows = pl.ds(at - MADE, LANES)
+        rest_ref[rows, :] = hot
+        copies.append(
+            pltpu.make_async_copy(rest_ref.at[rows], rest_hbm.at[rows], sems.at[len(copies)])
+        )
+        copies[-1].start()
+    beams = jnp.transpose(order_ref[...])
+    index = lax.broadcasted_iota(jnp.int32, (2 * CH_DEV, BEAMS), 1)
+    for pair in range(BEAMS // (2 * CH_DEV)):
+        columns = []
+        for g in RING[2 * pair : 2 * pair + 2]:
+            row = g * CH_DEV % LANES
+            at = g * CH_DEV // LANES
+            columns.append(beams[row : row + CH_DEV, at : at + 1])
+        turn_ref[pl.ds(pair * 2 * CH_DEV, 2 * CH_DEV), :] = jnp.where(
+            jnp.concatenate(columns, 0) == index, 1.0, 0.0
+        ).astype(jnp.bfloat16)
+    copies.append(pltpu.make_async_copy(turn_ref, turn_hbm, sems.at[len(copies)]))
+    copies[-1].start()
+    for copy in copies:
+        copy.wait()
+
+
+def one_hots(slots, beam_order, ids):
+    return pl.pallas_call(
+        one_hot_kernel,
+        in_specs=[IN_VMEM] * 3,
+        out_specs=[IN_VMEM, IN_HBM, IN_HBM],
+        out_shape=[
+            pltpu.VMEM((HEAD, INPUTS), jnp.bfloat16),
+            pltpu.HBM((INPUTS - MADE, INPUTS), jnp.bfloat16),
+            pltpu.HBM((BEAMS, BEAMS), jnp.bfloat16),
+        ],
+        scratch_shapes=[
+            pltpu.VMEM((INPUTS - MADE, INPUTS), jnp.bfloat16),
+            pltpu.VMEM((BEAMS, BEAMS), jnp.bfloat16),
+            pltpu.SemaphoreType.DMA(((INPUTS - MADE) // LANES + 1,)),
+        ],
+        compiler_params=pltpu.CompilerParams(vmem_limit_bytes=BEAM_VMEM),
+        cost_estimate=pl.CostEstimate(
+            flops=20 * 1024 * 1024, bytes_accessed=10 * 1024 * 1024, transcendentals=0
+        ),
+        name="one_hots",
+    )(
+        slots,
+        beam_order.reshape(BEAMS // LANES, LANES),
+        ids,
+    )
+
+
+def beam_kernel(
+    x_ref,
+    head_ref,
+    rest_hbm,
+    turn_hbm,
+    north_ref,
+    fine_ref,
+    slots_ref,
+    ids_ref,
+    out_ref,
+    made_ref,
+    rest_ref,
+    turn_ref,
+    fed_ref,
+    beam_ref,
+    power_ref,
+    sems,
+):
+    rest_copy = pltpu.make_async_copy(rest_hbm, rest_ref, sems.at[0])
+    turn_copy = pltpu.make_async_copy(turn_hbm, turn_ref, sems.at[1])
+    rest_copy.start()
+    turn_copy.start()
+    slots = jnp.transpose(slots_ref[...])
     for pol in range(POLS):
         for cyl in range(CYL):
-            rows = pl.ds((pol * CYL + cyl) * FEEDS, FEEDS)
-            fed_ref[rows, :] = jnp.dot(
-                pick_ref[rows, :], x_ref[...], preferred_element_type=jnp.float32
+            at = (pol * CYL + cyl) * FEEDS
+            if at < HEAD:
+                pick = head_ref[pl.ds(at, FEEDS), :]
+            elif at < MADE:
+                for block in range(at // LANES, (at + FEEDS) // LANES):
+                    made_ref[pl.ds(block * LANES - HEAD, LANES), :] = jnp.where(
+                        slots[:, block : block + 1] == ids_ref[...], 1.0, 0.0
+                    ).astype(jnp.bfloat16)
+                pick = made_ref[pl.ds(at - HEAD, FEEDS), :]
+            else:
+                if at == MADE:
+                    rest_copy.wait()
+                pick = rest_ref[pl.ds(at - MADE, FEEDS), :]
+            fed_ref[pl.ds(at, FEEDS), :] = jnp.dot(
+                pick, x_ref[...], preferred_element_type=jnp.float32
             ).astype(jnp.bfloat16)
         re, im = [], []
         for cyl in range(CYL):
@@ -311,28 +413,42 @@
             power_ref[...] = power
         else:
             total = (0.25 * (power_ref[...] + power)).astype(jnp.bfloat16)
+            turn_copy.wait()
             out_ref[...] = jnp.dot(
-                order_ref[...], total, preferred_element_type=jnp.float32
+                turn_ref[...], total, preferred_element_type=jnp.float32
             ).astype(jnp.bfloat16)
 
 
-def form_beams(piece, pick, order):
+def form_beams(piece, head, rest, turn, slots, ids):
     return pl.pallas_call(
         beam_kernel,
-        in_specs=[pl.BlockSpec(memory_space=pltpu.VMEM)] * 5,
-        out_specs=pl.BlockSpec(memory_space=pltpu.VMEM),
+        in_specs=[IN_VMEM, IN_VMEM, IN_HBM, IN_HBM, IN_VMEM, IN_VMEM, IN_VMEM, IN_VMEM],
+        out_specs=IN_VMEM,
         out_shape=jax.ShapeDtypeStruct((BEAMS, LANES), jnp.bfloat16),
         scratch_shapes=[
+            pltpu.VMEM((MADE - HEAD, INPUTS), jnp.bfloat16),
+            pltpu.VMEM((INPUTS - MADE, INPUTS), jnp.bfloat16),
+            pltpu.VMEM((BEAMS, BEAMS), jnp.bfloat16),
             pltpu.VMEM((INPUTS, 256), jnp.bfloat16),
             pltpu.VMEM((BEAMS, 256), jnp.bfloat16),
             pltpu.VMEM((BEAMS, LANES), jnp.float32),
+            pltpu.SemaphoreType.DMA((2,)),
         ],
         compiler_params=pltpu.CompilerParams(vmem_limit_bytes=BEAM_VMEM),
         cost_estimate=pl.CostEstimate(
             flops=2 * 1024 * 1024 * 1500, bytes_accessed=12 * 1024 * 1024, transcendentals=0
         ),
         name="form_beams",
-    )(piece, pick, order, jnp.asarray(north_table()), jnp.asarray(fine_table()))
+    )(
+        piece,
+        head,
+        pltpu.with_memory_space_constraint(rest, pltpu.HBM),
+        pltpu.with_memory_space_constraint(turn, pltpu.HBM),
+        jnp.asarray(north_table()),
+        jnp.asarray(fine_table()),
+        slots,
+        ids,
+    )
 
 
 def widen_kernel(x_ref, out_ref):
@@ -355,11 +471,13 @@
     prior = from_behind(tail, "ta", 1)
     held, window, table, later, picked = channelize_later(samples, gains)
     calibrated = channelize_first(held, prior, window, table, picked, later)
-    piece = lax.all_to_all(calibrated, "gx", split_axis=0, concat_axis=0, tiled=True)
-    pick = (slot_inputs[:, None] == jnp.arange(INPUTS, dtype=jnp.int32)[None, :]).astype(jnp.bfloat16)
-    order = (beam_order[:, None] == jnp.arange(BEAMS, dtype=jnp.int32)[None, :]).astype(jnp.bfloat16)
-    power = form_beams(piece, pick, order)
-    owned = lax.all_to_all(power, "gx", split_axis=0, concat_axis=0, tiled=True)
+    piece = exchange(calibrated)
+    ids = np.concatenate([np.arange(g * IN_DEV, (g + 1) * IN_DEV) for g in RING])
+    ids = jnp.asarray(ids[None, :], jnp.int32)
+    slots = slot_inputs.reshape(INPUTS // LANES, LANES)
+    head, rest, turn = one_hots(slots, beam_order, ids)
+    power = form_beams(piece, head, rest, turn, slots, ids)
+    owned = exchange(power)
     return widen(owned)
 
 

time: 91.1 us -> 84.7 us (0.930)
  other arithmetic: 5.05 us -> 0 us
  Pallas kernels: 12.9 us -> 17.4 us
  local copies, waits for them, and re-layouts: 4.35 us -> 0.97 us
  waiting for transfers between devices: 24.8 us -> 22.9 us
  blocking collectives: 23.7 us -> 22 us
    convert_element_type x2 -> x0, other arithmetic: 5.05 us -> none  [the longest x1 4.65 us: body(): (slot_inputs[:, None] == jnp.arange(INPUTS, dtype=jnp.int32)[None, :]).as...]
    pallas_call x1 -> x2, Pallas kernels: 4.59 us -> 9.15 us  [the longest x1 5.24 us: form_beams(): pl.pallas_call(beam_kernel, in_specs=[IN_VMEM, IN_VMEM, IN_HBM, IN_HBM, I...]
    unnamed x10, local copies, waits for them, and re-layouts: 3.41 us -> 0.03 us
    all_to_all x1, waiting for transfers between devices: 24.8 us -> 22.9 us  [exchange(): lax.all_to_all(block, 'gx', split_axis=0, concat_axis=0, axis_index_group...]
    all_to_all x1, blocking collectives: 23.7 us -> 22 us  [exchange(): lax.all_to_all(block, 'gx', split_axis=0, concat_axis=0, axis_index_group...]
  transfers between devices with their start and end apart: 2 -> 2, of which waited for: 1 -> 1; matrix products, arithmetic and copies ran while one was open for 6% -> 0% of each run, Pallas kernels for 4% -> 9%
where the time goes in v2:
time: 84.7 us; the launch traced here: 83.9 us
  waiting for transfers between devices  22.9 us (27%)
  blocking collectives  22 us (26%)
  starting transfers between devices  20.5 us (24%)
  Pallas kernels  17.4 us (21%)
  local copies, waits for them, and re-layouts  0.97 us (1%)
    all_to_all x1, waiting for transfers between devices, exchange(): lax.all_to_all(block, 'gx', split_axis=0, concat_axis=0, axis_index_group...  22.9 us
    all_to_all x1, blocking collectives, exchange(): lax.all_to_all(block, 'gx', split_axis=0, concat_axis=0, axis_index_group...  22 us
    all_to_all x1, starting transfers between devices, exchange(): lax.all_to_all(block, 'gx', split_axis=0, concat_axis=0, axis_index_group...  16.4 us
    pallas_call x1, Pallas kernels, form_beams(): pl.pallas_call(beam_kernel, in_specs=[IN_VMEM, IN_VMEM, IN_HBM, IN_HBM, I...  5.24 us
    ppermute x1, starting transfers between devices, from_behind(): return lax.ppermute(block, axis, route)  4.04 us
    pallas_call x1, Pallas kernels, one_hots(): pl.pallas_call(one_hot_kernel, in_specs=[IN_VMEM] * 3, out_specs=[IN_VMEM...  3.91 us
    pallas_call x1, Pallas kernels, channelize_later(): pl.pallas_call(later_kernel, in_specs=[IN_HBM] * 5, out_specs=[IN_VMEM] *...  3.77 us
    pallas_call x1, Pallas kernels, channelize_first(): pl.pallas_call(first_kernel, in_specs=[IN_VMEM] * 6, out_specs=IN_HBM, ou...  3.69 us
  transfers between devices with their start and end apart: 2, of which 1 were waited for; matrix products, arithmetic and copies ran while one was open for 0% of the time, Pallas kernels for 9%

profile of v2, /device:TPU:1, one launch (start us, length us, event | category | flops | bytes accessed | tf_op | source)
XLA Modules:
  0.0 83.9 jit_solution(4044145752554951596)
XLA Ops:
  0.0 0.9 %slice.3 = bf16[16,6144]{1,0:T(8,128)(2,1)S(1)} slice(bf16[16,32768]{1,0:T(8,128)(2,1)} %x_hbm.1), slice={[0:16], [26624:32768]} | slice | bytes 393216 | tf_op jit(solution)/shard_map/slice | solution.py:470
  0.9 4.0 %collective-permute-start = (bf16[16,6144]{1,0:T(8,128)(2,1)S(1)}, bf16[16,6144]{1,0:T(8,128)(2,1)S(1)}, u32[]{:S(2)}, u32[]{:S(2)}) collective-permute-start(bf16[16,6144]{1,0:T(8,128)(2,1)S(1)} %slice.3), channel_id=1, source_target_pairs={{0,1},{2,3},{4,5},{6,7},{8,9},{10,11},{12,13},{14,15},{16,17},{18,... | collective-permute-start | bytes 589832 | tf_op jit(solution)/shard_map/ppermute | solution.py:37
  5.0 3.8 %channelize_later.1 = (bf16[16,32768]{1,0:T(8,128)(2,1)S(1)}, f32[4,2048]{1,0:T(4,128)S(1)}, bf16[4,2,1024,256]{3,2,1,0:T(8,128)(2,1)S(1)}, bf16[4,2,2,208,128]{4,3,2,1,0:T(8,128)(2,1)S(1)}, f32[4,32,256]{2,1,0:T(8,128)S(1)}) custom-call(bf16[16,32768]{1,0:T(8,128)(2,1)} %x_hbm.1, f32[4,2048]{1,0:T(4,128)} %constant.12.clone.w_hbm, ...), custom_call_target="tpu_custom_call" | custom-call | flops 1073741824 | bytes 7340032 | tf_op jit(solution)/shard_map/channelize_later/pallas_call | solution.py:235
  8.8 0.0 collective-permute-done.prior_ref
  8.8 0.0 copy-start
  8.8 0.0 copy-start.1
  8.8 0.0 copy-start.4
  8.8 0.0 copy-start.2
  8.8 0.0 copy-start.3
  8.8 3.7 %channelize_first.1 = bf16[2048,256]{1,0:T(8,128)(2,1)} custom-call(bf16[16,32768]{1,0:T(8,128)(2,1)S(1)} %get-tuple-element.13.x_ref, bf16[16,6144]{1,0:T(8,128)(2,1)S(1)} %collective-permute-done.prior_ref, f32[4,2048]{1,0:T(4,128)S(1)} %get-tuple-element.14.w_ref, bf16[4,2,1024,256]{3,2,1,0:T(8,128)(2,1)S(1)} %get-tuple-element.15.t_ref, ...), custom_call_target="tpu_custom_call" | custom-call | flops 201326592 | bytes 7340032 | tf_op jit(solution)/shard_map/channelize_first/pallas_call | solution.py:272
  12.5 16.4 %all-to-all-start = ((bf16[128,16,256]{2,1,0:T(8,128)(2,1)}), bf16[128,16,256]{2,1,0:T(8,128)(2,1)S(1)}, u32[]{:S(2)}, u32[]{:S(2)}) async-start(bf16[128,16,256]{2,1,0:T(8,128)(2,1)} %bitcast), calls=%async_computation | async-start | bytes 2097152 | tf_op jit(solution)/shard_map/all_to_all | solution.py:41
  28.9 0.0 copy-done
  29.0 0.0 copy-done.1
  29.0 0.0 copy-done.4
  29.0 3.9 %one_hots.1 = (bf16[256,2048]{1,0:T(8,128)(2,1)S(1)}, bf16[1024,2048]{1,0:T(8,128)(2,1)}, bf16[1024,1024]{1,0:T(8,128)(2,1)}) custom-call(s32[16,128]{1,0:T(8,128)S(1)} %bitcast.7, s32[8,128]{1,0:T(8,128)S(1)} %bitcast.9, s32[1,2048]{1,0:T(1,128)S(1)} %copy-done.4), custom_call_target="tpu_custom_call" | custom-call | flops 20971520 | bytes 10485760 | tf_op jit(solution)/shard_map/one_hots/pallas_call | solution.py:323
  32.9 22.9 %all-to-all-done = bf16[128,16,256]{2,1,0:T(8,128)(2,1)S(1)} async-done(((bf16[128,16,256]{2,1,0:T(8,128)(2,1)}), bf16[128,16,256]{2,1,0:T(8,128)(2,1)S(1)}, u32[]{:S(2)}, u32[]{:S(2)}) %all-to-all-start) | async-done | bytes 1048608 | tf_op jit(solution)/shard_map/all_to_all | solution.py:41
  55.8 0.0 copy-done.2
  55.8 0.0 copy-done.3
  55.8 5.2 %form_beams.1 = bf16[1024,128]{1,0:T(8,128)(2,1)S(1)} custom-call(bf16[2048,256]{1,0:T(8,128)(2,1)S(1)} %bitcast.5, bf16[256,2048]{1,0:T(8,128)(2,1)S(1)} %get-tuple-element.18.head_ref, bf16[1024,2048]{1,0:T(8,128)(2,1)} %get-tuple-element.19.rest_hbm, bf16[1024,1024]{1,0:T(8,128)(2,1)} %get-tuple-element.20.turn_hbm, bf16[512,256]{1,0:T(8,128)(2,1)S(1)} %copy-done.2, ...), custom_call_target="tpu_custom_call" | custom-call | flops 3145728000 | bytes 12582912 | tf_op jit(solution)/shard_map/form_beams/pallas_call | solution.py:423
  61.1 22.0 %all_to_all.20.x_ref = bf16[128,8,128]{2,1,0:T(8,128)(2,1)S(1)} all-to-all(bf16[128,8,128]{2,1,0:T(8,128)(2,1)S(1)} %bitcast.6), channel_id=1, replica_groups={{70,16,226,68,10,84,176,234,146,116,30,12,34,160,50,206,46,140,118,248,..., dimensions={0} | all-to-all | bytes 524288 | tf_op jit(solution)/shard_map/all_to_all | solution.py:41
  83.1 0.8 widen.1
Async XLA Ops:
  0.9 7.8 %collective-permute-start = (bf16[16,6144]{1,0:T(8,128)(2,1)S(1)}, bf16[16,6144]{1,0:T(8,128)(2,1)S(1)}, u32[]{:S(2)}, u32[]{:S(2)}) collective-permute-start(bf16[16,6144]{1,0:T(8,128)(2,1)S(1)} %slice.3), channel_id=1, source_target_pairs={{0,1},{2,3},{4,5},{6,7},{8,9},{10,11},{12,13},{14,15},{16,17},{18,... | collective-permute-start | bytes 589832 | tf_op jit(solution)/shard_map/ppermute | solution.py:37
  8.8 20.2 %copy-start = (s32[2048]{0:T(1024)S(1)}, s32[2048]{0:T(1024)}, u32[]{:S(2)}) copy-start(s32[2048]{0:T(1024)} %param.12) | copy-start | bytes 24580
  8.8 20.2 %copy-start.1 = (s32[1024]{0:T(1024)S(1)}, s32[1024]{0:T(1024)}, u32[]{:S(2)}) copy-start(s32[1024]{0:T(1024)} %param.13) | copy-start | bytes 12292
  8.8 20.2 %copy-start.4 = (s32[1,2048]{1,0:T(1,128)S(1)}, s32[1,2048]{1,0:T(1,128)}, u32[]{:S(2)}) copy-start(s32[1,2048]{1,0:T(1,128)} %constant.15.clone.ids_ref) | copy-start | bytes 24580
  8.8 47.0 %copy-start.2 = (bf16[512,256]{1,0:T(8,128)(2,1)S(1)}, bf16[512,256]{1,0:T(8,128)(2,1)}, u32[]{:S(2)}) copy-start(bf16[512,256]{1,0:T(8,128)(2,1)} %constant.16.clone.north_ref) | copy-start | bytes 786436
  8.8 47.0 %copy-start.3 = (bf16[256,256]{1,0:T(8,128)(2,1)S(1)}, bf16[256,256]{1,0:T(8,128)(2,1)}, u32[]{:S(2)}) copy-start(bf16[256,256]{1,0:T(8,128)(2,1)} %constant.17.clone.fine_ref) | copy-start | bytes 393220
  12.5 43.3 %all-to-all-start = ((bf16[128,16,256]{2,1,0:T(8,128)(2,1)}), bf16[128,16,256]{2,1,0:T(8,128)(2,1)S(1)}, u32[]{:S(2)}, u32[]{:S(2)}) async-start(bf16[128,16,256]{2,1,0:T(8,128)(2,1)} %bitcast), calls=%async_computation | async-start | bytes 2097152 | tf_op jit(solution)/shard_map/all_to_all | solution.py:41

commit v3 on v2

--- a/solution.py
+++ b/solution.py
@@ -27,6 +27,7 @@
 ALL_VMEM = 40 * 1024 * 1024
 BEAM_VMEM = 32 * 1024 * 1024
 HEAD = 256
+ROWS = 64
 MADE = 1024
 RING = np.random.RandomState(3).permutation(128).tolist()
 
@@ -102,14 +103,16 @@
 def swap_groups(arrays):
     lane = lax.broadcasted_iota(jnp.int32, arrays[0].shape, 1) // 4
     arrays = list(arrays)
-    for bit in (16, 8, 4, 2, 1):
+    bit = len(arrays) // 2
+    while bit:
         low = (lane & bit) == 0
-        for j in range(32):
+        for j in range(len(arrays)):
             if j & bit:
                 continue
             a, b = arrays[j], arrays[j | bit]
             arrays[j] = jnp.where(low, a, pltpu.roll(b, 4 * bit, 1))
             arrays[j | bit] = jnp.where(low, pltpu.roll(a, LANES - 4 * bit, 1), b)
+        bit //= 2
     return arrays
 
 
@@ -183,26 +186,34 @@
         parts = jnp.concatenate([g_hi, g_mid, g_low], 0)
         picked = jnp.dot(parts, sel_ref[...], preferred_element_type=jnp.float32)
         picked_ref[block] = picked[0:32] + picked[32:64] + picked[64:96]
+    none = jnp.zeros((IN_DEV, LANES), jnp.bfloat16)
     for block in range(BLOCKS):
         copies[4 + block].wait()
         picked = picked_ref[block]
+        values = [[none] * 32, [none] * 32]
         for parity in range(2):
             lanes = slice(parity * LANES, (parity + 1) * LANES)
-            real, imag = calibrate(
+            late = calibrate(
                 z_ref[parity], t_ref[block, parity], picked[0:16, lanes], picked[16:32, lanes]
             )
-            for f in range(LATER):
-                rows = pl.ds(f * IN_DEV, IN_DEV)
-                out_ref[block, 0, parity, rows, :] = real[f].astype(jnp.bfloat16)
-                out_ref[block, 1, parity, rows, :] = imag[f].astype(jnp.bfloat16)
+            for part in range(2):
+                for f in range(LATER):
+                    values[part][2 * (f + TAPS - 1) + parity] = late[part][f].astype(jnp.bfloat16)
+        for part in range(2):
+            arrays = swap_groups(values[part])
+            for d in range(32):
+                rows = pl.ds((block * 32 + d) * IN_DEV, IN_DEV)
+                out_ref[rows, pl.ds(part * LANES, LANES)] = arrays[d]
 
 
 def first_kernel(x_ref, prior_ref, w_ref, t_ref, picked_ref, later_ref, out_hbm, z_ref, out_ref, sems):
     fold_frames([prior_ref, x_ref.at[:, : (TAPS - 1) * FRAME]], w_ref, z_ref, TAPS - 1)
+    none = jnp.zeros((IN_DEV, LANES), jnp.bfloat16)
+    is_early = lax.broadcasted_iota(jnp.int32, (IN_DEV, LANES), 1) < CH_DEV * (TAPS - 1)
     copies = []
     for block in range(BLOCKS):
         picked = picked_ref[block]
-        values = [[None] * 32, [None] * 32]
+        values = [[none] * 8, [none] * 8]
         for parity in range(2):
             lanes = slice(parity * LANES, (parity + 1) * LANES)
             early = calibrate(
@@ -211,14 +222,15 @@
             for part in range(2):
                 for f in range(TAPS - 1):
                     values[part][2 * f + parity] = early[part][f].astype(jnp.bfloat16)
-                for f in range(LATER):
-                    rows = pl.ds(f * IN_DEV, IN_DEV)
-                    values[part][2 * (f + TAPS - 1) + parity] = later_ref[block, part, parity, rows, :]
         for part in range(2):
             arrays = swap_groups(values[part])
             for d in range(32):
                 rows = pl.ds((block * 32 + d) * IN_DEV, IN_DEV)
-                out_ref[rows, pl.ds(part * LANES, LANES)] = arrays[d]
+                lanes = pl.ds(part * LANES, LANES)
+                moved = arrays[d % 8]
+                if d >= 8:
+                    moved = pltpu.roll(moved, LANES - 32 * (d // 8), 1)
+                out_ref[rows, lanes] = jnp.where(is_early, moved, later_ref[rows, lanes])
         rows = pl.ds(block * 32 * IN_DEV, 32 * IN_DEV)
         copies.append(pltpu.make_async_copy(out_ref.at[rows], out_hbm.at[rows], sems.at[block]))
         copies[block].start()
@@ -240,7 +252,7 @@
             pltpu.VMEM((IN_DEV, F_DEV * FRAME), jnp.bfloat16),
             pltpu.VMEM((TAPS, FRAME), jnp.float32),
             pltpu.VMEM(table.shape, jnp.bfloat16),
-            pltpu.VMEM((BLOCKS, 2, 2, LATER * IN_DEV, LANES), jnp.bfloat16),
+            pltpu.VMEM((INPUTS, 256), jnp.bfloat16),
             pltpu.VMEM((BLOCKS, 2 * IN_DEV, 2 * LANES), jnp.float32),
         ],
         scratch_shapes=[
@@ -360,8 +372,10 @@
     rest_ref,
     turn_ref,
     fed_ref,
+    north_out_ref,
     beam_ref,
     power_ref,
+    total_ref,
     sems,
 ):
     rest_copy = pltpu.make_async_copy(rest_hbm, rest_ref, sems.at[0])
@@ -369,54 +383,72 @@
     rest_copy.start()
     turn_copy.start()
     slots = jnp.transpose(slots_ref[...])
-    for pol in range(POLS):
-        for cyl in range(CYL):
-            at = (pol * CYL + cyl) * FEEDS
-            if at < HEAD:
-                pick = head_ref[pl.ds(at, FEEDS), :]
-            elif at < MADE:
-                for block in range(at // LANES, (at + FEEDS) // LANES):
-                    made_ref[pl.ds(block * LANES - HEAD, LANES), :] = jnp.where(
-                        slots[:, block : block + 1] == ids_ref[...], 1.0, 0.0
-                    ).astype(jnp.bfloat16)
-                pick = made_ref[pl.ds(at - HEAD, FEEDS), :]
-            else:
-                if at == MADE:
-                    rest_copy.wait()
-                pick = rest_ref[pl.ds(at - MADE, FEEDS), :]
-            fed_ref[pl.ds(at, FEEDS), :] = jnp.dot(
-                pick, x_ref[...], preferred_element_type=jnp.float32
-            ).astype(jnp.bfloat16)
-        re, im = [], []
-        for cyl in range(CYL):
-            rows = pl.ds((pol * CYL + cyl) * FEEDS, FEEDS)
-            both = jnp.dot(north_ref[...], fed_ref[rows, :], preferred_element_type=jnp.float32)
-            re.append(both[:FEEDS, :LANES] + both[FEEDS:, LANES:])
-            im.append(both[:FEEDS, LANES:] - both[FEEDS:, :LANES])
+    def feed(step):
+        at = step * FEEDS
+        if at < HEAD:
+            pick = head_ref[pl.ds(at, FEEDS), :]
+        elif at < MADE:
+            for block in range(at // LANES, (at + FEEDS) // LANES):
+                made_ref[pl.ds(block * LANES - HEAD, LANES), :] = jnp.where(
+                    slots[:, block : block + 1] == ids_ref[...], 1.0, 0.0
+                ).astype(jnp.bfloat16)
+            pick = made_ref[pl.ds(at - HEAD, FEEDS), :]
+        else:
+            if at == MADE:
+                rest_copy.wait()
+            pick = rest_ref[pl.ds(at - MADE, FEEDS), :]
+        fed_ref[pl.ds(at, FEEDS), :] = jnp.dot(
+            pick, x_ref[...], preferred_element_type=jnp.float32
+        ).astype(jnp.bfloat16)
+
+    def north(step):
+        rows = pl.ds(step * FEEDS, FEEDS)
+        both = jnp.dot(north_ref[...], fed_ref[rows, :], preferred_element_type=jnp.float32)
+        north_out_ref[step, 0] = both[:FEEDS, :LANES] + both[FEEDS:, LANES:]
+        north_out_ref[step, 1] = both[:FEEDS, LANES:] - both[FEEDS:, :LANES]
+
+    def east(pol, row):
+        rows = pl.ds(row, ROWS)
+        re = [north_out_ref[pol * CYL + c, 0, rows, :] for c in range(CYL)]
+        im = [north_out_ref[pol * CYL + c, 1, rows, :] for c in range(CYL)]
         sum_re, dif_re = re[0] + re[2], re[0] - re[2]
         sum_im, dif_im = im[0] + im[2], im[0] - im[2]
         odd_re, odd_dif_re = re[1] + re[3], re[1] - re[3]
         odd_im, odd_dif_im = im[1] + im[3], im[1] - im[3]
-        east = (
+        out = (
             (sum_re + odd_re, sum_im + odd_im),
             (dif_re + odd_dif_im, dif_im - odd_dif_re),
             (sum_re - odd_re, sum_im - odd_im),
             (dif_re - odd_dif_im, dif_im + odd_dif_re),
         )
         for e in range(CYL):
-            beam_ref[pl.ds(e * FEEDS, FEEDS), :LANES] = east[e][0].astype(jnp.bfloat16)
-            beam_ref[pl.ds(e * FEEDS, FEEDS), LANES:] = east[e][1].astype(jnp.bfloat16)
-        fine = jnp.dot(beam_ref[...], fine_ref[...], preferred_element_type=jnp.float32)
+            at = pl.ds(e * FEEDS + row, ROWS)
+            beam_ref[at, :LANES] = out[e][0].astype(jnp.bfloat16)
+            beam_ref[at, LANES:] = out[e][1].astype(jnp.bfloat16)
+
+    def detect(pol, e):
+        rows = pl.ds(e * FEEDS, FEEDS)
+        fine = jnp.dot(beam_ref[rows, :], fine_ref[...], preferred_element_type=jnp.float32)
         squares = fine * fine
         power = squares[:, :LANES] + squares[:, LANES:]
         if pol == 0:
-            power_ref[...] = power
+            power_ref[rows, :] = power
         else:
-            total = (0.25 * (power_ref[...] + power)).astype(jnp.bfloat16)
-            turn_copy.wait()
-            out_ref[...] = jnp.dot(
-                turn_ref[...], total, preferred_element_type=jnp.float32
-            ).astype(jnp.bfloat16)
+            total_ref[rows, :] = (0.25 * (power_ref[rows, :] + power)).astype(jnp.bfloat16)
+
+    for pol in range(POLS):
+        for cyl in range(CYL):
+            feed(pol * CYL + cyl)
+        for cyl in range(CYL):
+            north(pol * CYL + cyl)
+        for row in range(0, FEEDS, ROWS):
+            east(pol, row)
+        for e in range(CYL):
+            detect(pol, e)
+    turn_copy.wait()
+    out_ref[...] = jnp.dot(
+        turn_ref[...], total_ref[...], preferred_element_type=jnp.float32
+    ).astype(jnp.bfloat16)
 
 
 def form_beams(piece, head, rest, turn, slots, ids):
@@ -430,8 +462,10 @@
             pltpu.VMEM((INPUTS - MADE, INPUTS), jnp.bfloat16),
             pltpu.VMEM((BEAMS, BEAMS), jnp.bfloat16),
             pltpu.VMEM((INPUTS, 256), jnp.bfloat16),
+            pltpu.VMEM((POLS * CYL, 2, FEEDS, LANES), jnp.float32),
             pltpu.VMEM((BEAMS, 256), jnp.bfloat16),
             pltpu.VMEM((BEAMS, LANES), jnp.float32),
+            pltpu.VMEM((BEAMS, LANES), jnp.bfloat16),
             pltpu.SemaphoreType.DMA((2,)),
         ],
         compiler_params=pltpu.CompilerParams(vmem_limit_bytes=BEAM_VMEM),

time: 84.7 us -> 83.4 us (0.985)
    pallas_call x1, Pallas kernels: 3.77 us -> 5.35 us  [channelize_later(): pl.pallas_call(later_kernel, in_specs=[IN_HBM] * 5, out_specs=[IN_VMEM] *...]
    pallas_call x1, Pallas kernels: 3.69 us -> 2.13 us  [channelize_first(): pl.pallas_call(first_kernel, in_specs=[IN_VMEM] * 6, out_specs=IN_HBM, ou...]
  transfers between devices with their start and end apart: 2 -> 2, of which waited for: 1 -> 1; matrix products, arithmetic and copies ran while one was open for 0% -> 0% of each run, Pallas kernels for 9% -> 11%
where the time goes in v3:
time: 83.4 us; the launch traced here: 83.2 us
  waiting for transfers between devices  22.9 us (27%)
  blocking collectives  22 us (26%)
  starting transfers between devices  20.1 us (24%)
  Pallas kernels  17 us (20%)
  local copies, waits for them, and re-layouts  0.97 us (1%)
    all_to_all x1, waiting for transfers between devices, exchange(): lax.all_to_all(block, 'gx', split_axis=0, concat_axis=0, axis_index_group...  22.9 us
    all_to_all x1, blocking collectives, exchange(): lax.all_to_all(block, 'gx', split_axis=0, concat_axis=0, axis_index_group...  22 us
    all_to_all x1, starting transfers between devices, exchange(): lax.all_to_all(block, 'gx', split_axis=0, concat_axis=0, axis_index_group...  16.1 us
    pallas_call x1, Pallas kernels, channelize_later(): pl.pallas_call(later_kernel, in_specs=[IN_HBM] * 5, out_specs=[IN_VMEM] *...  5.35 us
    pallas_call x1, Pallas kernels, form_beams(): pl.pallas_call(beam_kernel, in_specs=[IN_VMEM, IN_VMEM, IN_HBM, IN_HBM, I...  4.77 us
    ppermute x1, starting transfers between devices, from_behind(): return lax.ppermute(block, axis, route)  4.04 us
    pallas_call x1, Pallas kernels, one_hots(): pl.pallas_call(one_hot_kernel, in_specs=[IN_VMEM] * 3, out_specs=[IN_VMEM...  3.91 us
    pallas_call x1, Pallas kernels, channelize_first(): pl.pallas_call(first_kernel, in_specs=[IN_VMEM] * 6, out_specs=IN_HBM, ou...  2.13 us
  transfers between devices with their start and end apart: 2, of which 1 were waited for; matrix products, arithmetic and copies ran while one was open for 0% of the time, Pallas kernels for 11%

profile of v3, /device:TPU:1, one launch (start us, length us, event | category | flops | bytes accessed | tf_op | source)
XLA Modules:
  0.0 83.2 jit_solution(17327348100484618181)
XLA Ops:
  0.0 0.9 %slice.3 = bf16[16,6144]{1,0:T(8,128)(2,1)S(1)} slice(bf16[16,32768]{1,0:T(8,128)(2,1)} %x_hbm.1), slice={[0:16], [26624:32768]} | slice | bytes 393216 | tf_op jit(solution)/shard_map/slice | solution.py:504
  0.9 4.0 %collective-permute-start = (bf16[16,6144]{1,0:T(8,128)(2,1)S(1)}, bf16[16,6144]{1,0:T(8,128)(2,1)S(1)}, u32[]{:S(2)}, u32[]{:S(2)}) collective-permute-start(bf16[16,6144]{1,0:T(8,128)(2,1)S(1)} %slice.3), channel_id=1, source_target_pairs={{0,1},{2,3},{4,5},{6,7},{8,9},{10,11},{12,13},{14,15},{16,17},{18,... | collective-permute-start | bytes 589832 | tf_op jit(solution)/shard_map/ppermute | solution.py:38
  5.0 5.4 %channelize_later.1 = (bf16[16,32768]{1,0:T(8,128)(2,1)S(1)}, f32[4,2048]{1,0:T(4,128)S(1)}, bf16[4,2,1024,256]{3,2,1,0:T(8,128)(2,1)S(1)}, bf16[2048,256]{1,0:T(8,128)(2,1)S(1)}, f32[4,32,256]{2,1,0:T(8,128)S(1)}) custom-call(bf16[16,32768]{1,0:T(8,128)(2,1)} %x_hbm.1, f32[4,2048]{1,0:T(4,128)} %constant.12.clone.w_hbm, ...), custom_call_target="tpu_custom_call" | custom-call | flops 1073741824 | bytes 7340032 | tf_op jit(solution)/shard_map/channelize_later/pallas_call | solution.py:247
  10.4 0.0 collective-permute-done.prior_ref
  10.4 0.0 copy-start
  10.4 0.0 copy-start.1
  10.4 0.0 copy-start.4
  10.4 0.0 copy-start.2
  10.4 0.0 copy-start.3
  10.4 2.1 %channelize_first.1 = bf16[2048,256]{1,0:T(8,128)(2,1)} custom-call(bf16[16,32768]{1,0:T(8,128)(2,1)S(1)} %get-tuple-element.13.x_ref, bf16[16,6144]{1,0:T(8,128)(2,1)S(1)} %collective-permute-done.prior_ref, f32[4,2048]{1,0:T(4,128)S(1)} %get-tuple-element.14.w_ref, bf16[4,2,1024,256]{3,2,1,0:T(8,128)(2,1)S(1)} %get-tuple-element.15.t_ref, ...), custom_call_target="tpu_custom_call" | custom-call | flops 201326592 | bytes 7340032 | tf_op jit(solution)/shard_map/channelize_first/pallas_call | solution.py:284
  12.6 16.1 %all-to-all-start = ((bf16[128,16,256]{2,1,0:T(8,128)(2,1)}), bf16[128,16,256]{2,1,0:T(8,128)(2,1)S(1)}, u32[]{:S(2)}, u32[]{:S(2)}) async-start(bf16[128,16,256]{2,1,0:T(8,128)(2,1)} %bitcast), calls=%async_computation | async-start | bytes 2097152 | tf_op jit(solution)/shard_map/all_to_all | solution.py:42
  28.7 0.0 copy-done
  28.7 0.0 copy-done.1
  28.7 0.0 copy-done.4
  28.7 3.9 %one_hots.1 = (bf16[256,2048]{1,0:T(8,128)(2,1)S(1)}, bf16[1024,2048]{1,0:T(8,128)(2,1)}, bf16[1024,1024]{1,0:T(8,128)(2,1)}) custom-call(s32[16,128]{1,0:T(8,128)S(1)} %bitcast.7, s32[8,128]{1,0:T(8,128)S(1)} %bitcast.9, s32[1,2048]{1,0:T(1,128)S(1)} %copy-done.4), custom_call_target="tpu_custom_call" | custom-call | flops 20971520 | bytes 10485760 | tf_op jit(solution)/shard_map/one_hots/pallas_call | solution.py:335
  32.6 22.9 %all-to-all-done = bf16[128,16,256]{2,1,0:T(8,128)(2,1)S(1)} async-done(((bf16[128,16,256]{2,1,0:T(8,128)(2,1)}), bf16[128,16,256]{2,1,0:T(8,128)(2,1)S(1)}, u32[]{:S(2)}, u32[]{:S(2)}) %all-to-all-start) | async-done | bytes 1048608 | tf_op jit(solution)/shard_map/all_to_all | solution.py:42
  55.6 0.0 copy-done.2
  55.6 0.0 copy-done.3
  55.6 4.8 %form_beams.1 = bf16[1024,128]{1,0:T(8,128)(2,1)S(1)} custom-call(bf16[2048,256]{1,0:T(8,128)(2,1)S(1)} %bitcast.5, bf16[256,2048]{1,0:T(8,128)(2,1)S(1)} %get-tuple-element.18.head_ref, bf16[1024,2048]{1,0:T(8,128)(2,1)} %get-tuple-element.19.rest_hbm, bf16[1024,1024]{1,0:T(8,128)(2,1)} %get-tuple-element.20.turn_hbm, bf16[512,256]{1,0:T(8,128)(2,1)S(1)} %copy-done.2, ...), custom_call_target="tpu_custom_call" | custom-call | flops 3145728000 | bytes 12582912 | tf_op jit(solution)/shard_map/form_beams/pallas_call | solution.py:455
  60.3 22.0 %all_to_all.20.x_ref = bf16[128,8,128]{2,1,0:T(8,128)(2,1)S(1)} all-to-all(bf16[128,8,128]{2,1,0:T(8,128)(2,1)S(1)} %bitcast.6), channel_id=1, replica_groups={{70,16,226,68,10,84,176,234,146,116,30,12,34,160,50,206,46,140,118,248,..., dimensions={0} | all-to-all | bytes 524288 | tf_op jit(solution)/shard_map/all_to_all | solution.py:42
  82.4 0.8 widen.1
Async XLA Ops:
  0.9 9.4 %collective-permute-start = (bf16[16,6144]{1,0:T(8,128)(2,1)S(1)}, bf16[16,6144]{1,0:T(8,128)(2,1)S(1)}, u32[]{:S(2)}, u32[]{:S(2)}) collective-permute-start(bf16[16,6144]{1,0:T(8,128)(2,1)S(1)} %slice.3), channel_id=1, source_target_pairs={{0,1},{2,3},{4,5},{6,7},{8,9},{10,11},{12,13},{14,15},{16,17},{18,... | collective-permute-start | bytes 589832 | tf_op jit(solution)/shard_map/ppermute | solution.py:38
  10.4 18.3 %copy-start = (s32[2048]{0:T(1024)S(1)}, s32[2048]{0:T(1024)}, u32[]{:S(2)}) copy-start(s32[2048]{0:T(1024)} %param.12) | copy-start | bytes 24580
  10.4 18.3 %copy-start.1 = (s32[1024]{0:T(1024)S(1)}, s32[1024]{0:T(1024)}, u32[]{:S(2)}) copy-start(s32[1024]{0:T(1024)} %param.13) | copy-start | bytes 12292
  10.4 18.3 %copy-start.4 = (s32[1,2048]{1,0:T(1,128)S(1)}, s32[1,2048]{1,0:T(1,128)}, u32[]{:S(2)}) copy-start(s32[1,2048]{1,0:T(1,128)} %constant.15.clone.ids_ref) | copy-start | bytes 24580
  10.4 45.2 %copy-start.2 = (bf16[512,256]{1,0:T(8,128)(2,1)S(1)}, bf16[512,256]{1,0:T(8,128)(2,1)}, u32[]{:S(2)}) copy-start(bf16[512,256]{1,0:T(8,128)(2,1)} %constant.16.clone.north_ref) | copy-start | bytes 786436
  10.4 45.1 %copy-start.3 = (bf16[256,256]{1,0:T(8,128)(2,1)S(1)}, bf16[256,256]{1,0:T(8,128)(2,1)}, u32[]{:S(2)}) copy-start(bf16[256,256]{1,0:T(8,128)(2,1)} %constant.17.clone.fine_ref) | copy-start | bytes 393220
  12.6 43.0 %all-to-all-start = ((bf16[128,16,256]{2,1,0:T(8,128)(2,1)}), bf16[128,16,256]{2,1,0:T(8,128)(2,1)S(1)}, u32[]{:S(2)}, u32[]{:S(2)}) async-start(bf16[128,16,256]{2,1,0:T(8,128)(2,1)} %bitcast), calls=%async_computation | async-start | bytes 2097152 | tf_op jit(solution)/shard_map/all_to_all | solution.py:42

commit v4 on v3

--- a/solution.py
+++ b/solution.py
@@ -29,7 +29,7 @@
 HEAD = 256
 ROWS = 64
 MADE = 1024
-RING = np.random.RandomState(3).permutation(128).tolist()
+RING = list(range(INPUTS // IN_DEV))[::-1]
 
 
 def from_behind(block, axis, distance):

time: 83.4 us -> 81.1 us (0.972)
  waiting for transfers between devices: 22.9 us -> 20.3 us
    all_to_all x1, waiting for transfers between devices: 22.9 us -> 20.3 us  [exchange(): lax.all_to_all(block, 'gx', split_axis=0, concat_axis=0, axis_index_group...]
where the time goes in v4:
time: 81.1 us; the launch traced here: 80.9 us
  blocking collectives  22.2 us (27%)
  starting transfers between devices  20.9 us (26%)
  waiting for transfers between devices  20.3 us (25%)
  Pallas kernels  16.3 us (20%)
  local copies, waits for them, and re-layouts  0.97 us (1%)
    all_to_all x1, blocking collectives, exchange(): lax.all_to_all(block, 'gx', split_axis=0, concat_axis=0, axis_index_group...  22.2 us
    all_to_all x1, waiting for transfers between devices, exchange(): lax.all_to_all(block, 'gx', split_axis=0, concat_axis=0, axis_index_group...  20.3 us
    all_to_all x1, starting transfers between devices, exchange(): lax.all_to_all(block, 'gx', split_axis=0, concat_axis=0, axis_index_group...  16.8 us
    pallas_call x1, Pallas kernels, channelize_later(): pl.pallas_call(later_kernel, in_specs=[IN_HBM] * 5, out_specs=[IN_VMEM] *...  5.35 us
    pallas_call x1, Pallas kernels, form_beams(): pl.pallas_call(beam_kernel, in_specs=[IN_VMEM, IN_VMEM, IN_HBM, IN_HBM, I...  4.76 us
    ppermute x1, starting transfers between devices, from_behind(): return lax.ppermute(block, axis, route)  4.04 us
    pallas_call x1, Pallas kernels, one_hots(): pl.pallas_call(one_hot_kernel, in_specs=[IN_VMEM] * 3, out_specs=[IN_VMEM...  3.24 us
    pallas_call x1, Pallas kernels, channelize_first(): pl.pallas_call(first_kernel, in_specs=[IN_VMEM] * 6, out_specs=IN_HBM, ou...  2.13 us
  transfers between devices with their start and end apart: 2, of which 1 were waited for; matrix products, arithmetic and copies ran while one was open for 0% of the time, Pallas kernels for 11%

profile of v4, /device:TPU:1, one launch (start us, length us, event | category | flops | bytes accessed | tf_op | source)
XLA Modules:
  0.0 80.9 jit_solution(13452685958267734478)
XLA Ops:
  0.0 0.9 %slice.3 = bf16[16,6144]{1,0:T(8,128)(2,1)S(1)} slice(bf16[16,32768]{1,0:T(8,128)(2,1)} %x_hbm.1), slice={[0:16], [26624:32768]} | slice | bytes 393216 | tf_op jit(solution)/shard_map/slice | solution.py:504
  0.9 4.0 %collective-permute-start = (bf16[16,6144]{1,0:T(8,128)(2,1)S(1)}, bf16[16,6144]{1,0:T(8,128)(2,1)S(1)}, u32[]{:S(2)}, u32[]{:S(2)}) collective-permute-start(bf16[16,6144]{1,0:T(8,128)(2,1)S(1)} %slice.3), channel_id=1, source_target_pairs={{0,1},{2,3},{4,5},{6,7},{8,9},{10,11},{12,13},{14,15},{16,17},{18,... | collective-permute-start | bytes 589832 | tf_op jit(solution)/shard_map/ppermute | solution.py:38
  5.0 5.4 %channelize_later.1 = (bf16[16,32768]{1,0:T(8,128)(2,1)S(1)}, f32[4,2048]{1,0:T(4,128)S(1)}, bf16[4,2,1024,256]{3,2,1,0:T(8,128)(2,1)S(1)}, bf16[2048,256]{1,0:T(8,128)(2,1)S(1)}, f32[4,32,256]{2,1,0:T(8,128)S(1)}) custom-call(bf16[16,32768]{1,0:T(8,128)(2,1)} %x_hbm.1, f32[4,2048]{1,0:T(4,128)} %constant.12.clone.w_hbm, ...), custom_call_target="tpu_custom_call" | custom-call | flops 1073741824 | bytes 7340032 | tf_op jit(solution)/shard_map/channelize_later/pallas_call | solution.py:247
  10.4 0.0 collective-permute-done.prior_ref
  10.4 0.0 copy-start
  10.4 0.0 copy-start.1
  10.4 0.0 copy-start.4
  10.4 0.0 copy-start.2
  10.4 0.0 copy-start.3
  10.4 2.1 %channelize_first.1 = bf16[2048,256]{1,0:T(8,128)(2,1)} custom-call(bf16[16,32768]{1,0:T(8,128)(2,1)S(1)} %get-tuple-element.13.x_ref, bf16[16,6144]{1,0:T(8,128)(2,1)S(1)} %collective-permute-done.prior_ref, f32[4,2048]{1,0:T(4,128)S(1)} %get-tuple-element.14.w_ref, bf16[4,2,1024,256]{3,2,1,0:T(8,128)(2,1)S(1)} %get-tuple-element.15.t_ref, ...), custom_call_target="tpu_custom_call" | custom-call | flops 201326592 | bytes 7340032 | tf_op jit(solution)/shard_map/channelize_first/pallas_call | solution.py:284
  12.6 16.8 %all-to-all-start = ((bf16[128,16,256]{2,1,0:T(8,128)(2,1)}), bf16[128,16,256]{2,1,0:T(8,128)(2,1)S(1)}, u32[]{:S(2)}, u32[]{:S(2)}) async-start(bf16[128,16,256]{2,1,0:T(8,128)(2,1)} %bitcast), calls=%async_computation | async-start | bytes 2097152 | tf_op jit(solution)/shard_map/all_to_all | solution.py:42
  29.4 0.0 copy-done
  29.4 0.0 copy-done.1
  29.4 0.0 copy-done.4
  29.4 3.2 %one_hots.1 = (bf16[256,2048]{1,0:T(8,128)(2,1)S(1)}, bf16[1024,2048]{1,0:T(8,128)(2,1)}, bf16[1024,1024]{1,0:T(8,128)(2,1)}) custom-call(s32[16,128]{1,0:T(8,128)S(1)} %bitcast.7, s32[8,128]{1,0:T(8,128)S(1)} %bitcast.9, s32[1,2048]{1,0:T(1,128)S(1)} %copy-done.4), custom_call_target="tpu_custom_call" | custom-call | flops 20971520 | bytes 10485760 | tf_op jit(solution)/shard_map/one_hots/pallas_call | solution.py:335
  32.7 20.3 %all-to-all-done = bf16[128,16,256]{2,1,0:T(8,128)(2,1)S(1)} async-done(((bf16[128,16,256]{2,1,0:T(8,128)(2,1)}), bf16[128,16,256]{2,1,0:T(8,128)(2,1)S(1)}, u32[]{:S(2)}, u32[]{:S(2)}) %all-to-all-start) | async-done | bytes 1048608 | tf_op jit(solution)/shard_map/all_to_all | solution.py:42
  53.0 0.0 copy-done.2
  53.0 0.0 copy-done.3
  53.0 4.8 %form_beams.1 = bf16[1024,128]{1,0:T(8,128)(2,1)S(1)} custom-call(bf16[2048,256]{1,0:T(8,128)(2,1)S(1)} %bitcast.5, bf16[256,2048]{1,0:T(8,128)(2,1)S(1)} %get-tuple-element.18.head_ref, bf16[1024,2048]{1,0:T(8,128)(2,1)} %get-tuple-element.19.rest_hbm, bf16[1024,1024]{1,0:T(8,128)(2,1)} %get-tuple-element.20.turn_hbm, bf16[512,256]{1,0:T(8,128)(2,1)S(1)} %copy-done.2, ...), custom_call_target="tpu_custom_call" | custom-call | flops 3145728000 | bytes 12582912 | tf_op jit(solution)/shard_map/form_beams/pallas_call | solution.py:455
  57.8 22.2 %all_to_all.20.x_ref = bf16[128,8,128]{2,1,0:T(8,128)(2,1)S(1)} all-to-all(bf16[128,8,128]{2,1,0:T(8,128)(2,1)S(1)} %bitcast.6), channel_id=1, replica_groups={{254,252,250,248,246,244,242,240,238,236,234,232,230,228,226,224,222,22..., dimensions={0} | all-to-all | bytes 524288 | tf_op jit(solution)/shard_map/all_to_all | solution.py:42
  80.0 0.8 %widen.1 = f32[1,8,16384]{2,1,0:T(8,128)} custom-call(bf16[128,8,128]{2,1,0:T(8,128)(2,1)S(1)} %all_to_all.20.x_ref), custom_call_target="tpu_custom_call" | custom-call | tf_op jit(solution)/shard_map/widen/pallas_call | solution.py:495
Async XLA Ops:
  0.9 9.4 %collective-permute-start = (bf16[16,6144]{1,0:T(8,128)(2,1)S(1)}, bf16[16,6144]{1,0:T(8,128)(2,1)S(1)}, u32[]{:S(2)}, u32[]{:S(2)}) collective-permute-start(bf16[16,6144]{1,0:T(8,128)(2,1)S(1)} %slice.3), channel_id=1, source_target_pairs={{0,1},{2,3},{4,5},{6,7},{8,9},{10,11},{12,13},{14,15},{16,17},{18,... | collective-permute-start | bytes 589832 | tf_op jit(solution)/shard_map/ppermute | solution.py:38
  10.4 19.1 %copy-start = (s32[2048]{0:T(1024)S(1)}, s32[2048]{0:T(1024)}, u32[]{:S(2)}) copy-start(s32[2048]{0:T(1024)} %param.12) | copy-start | bytes 24580
  10.4 19.1 %copy-start.1 = (s32[1024]{0:T(1024)S(1)}, s32[1024]{0:T(1024)}, u32[]{:S(2)}) copy-start(s32[1024]{0:T(1024)} %param.13) | copy-start | bytes 12292
  10.4 19.1 %copy-start.4 = (s32[1,2048]{1,0:T(1,128)S(1)}, s32[1,2048]{1,0:T(1,128)}, u32[]{:S(2)}) copy-start(s32[1,2048]{1,0:T(1,128)} %constant.15.clone.ids_ref) | copy-start | bytes 24580
  10.4 42.6 %copy-start.2 = (bf16[512,256]{1,0:T(8,128)(2,1)S(1)}, bf16[512,256]{1,0:T(8,128)(2,1)}, u32[]{:S(2)}) copy-start(bf16[512,256]{1,0:T(8,128)(2,1)} %constant.16.clone.north_ref) | copy-start | bytes 786436
  10.4 42.6 %copy-start.3 = (bf16[256,256]{1,0:T(8,128)(2,1)S(1)}, bf16[256,256]{1,0:T(8,128)(2,1)}, u32[]{:S(2)}) copy-start(bf16[256,256]{1,0:T(8,128)(2,1)} %constant.17.clone.fine_ref) | copy-start | bytes 393220
  12.6 40.5 %all-to-all-start = ((bf16[128,16,256]{2,1,0:T(8,128)(2,1)}), bf16[128,16,256]{2,1,0:T(8,128)(2,1)S(1)}, u32[]{:S(2)}, u32[]{:S(2)}) async-start(bf16[128,16,256]{2,1,0:T(8,128)(2,1)} %bitcast), calls=%async_computation | async-start | bytes 2097152 | tf_op jit(solution)/shard_map/all_to_all | solution.py:42

commit v5 on v4

--- a/solution.py
+++ b/solution.py
@@ -29,7 +29,7 @@
 HEAD = 256
 ROWS = 64
 MADE = 1024
-RING = list(range(INPUTS // IN_DEV))[::-1]
+RING = [x * 32 + z * 4 + k for x in (3, 2, 1, 0) for z in (7, 3, 6, 2, 5, 1, 4, 0) for k in (3, 2, 1, 0)]
 
 
 def from_behind(block, axis, distance):

time: 81.1 us -> 80.4 us (level)
  no operation moved by 1% of the time
where the time goes in v5:
time: 80.4 us; the launch traced here: 80.1 us
  blocking collectives  22 us (27%)
  starting transfers between devices  20.9 us (26%)
  waiting for transfers between devices  19.8 us (25%)
  Pallas kernels  16.3 us (20%)
  local copies, waits for them, and re-layouts  0.97 us (1%)
    all_to_all x1, blocking collectives, exchange(): lax.all_to_all(block, 'gx', split_axis=0, concat_axis=0, axis_index_group...  22 us
    all_to_all x1, waiting for transfers between devices, exchange(): lax.all_to_all(block, 'gx', split_axis=0, concat_axis=0, axis_index_group...  19.8 us
    all_to_all x1, starting transfers between devices, exchange(): lax.all_to_all(block, 'gx', split_axis=0, concat_axis=0, axis_index_group...  16.8 us
    pallas_call x1, Pallas kernels, channelize_later(): pl.pallas_call(later_kernel, in_specs=[IN_HBM] * 5, out_specs=[IN_VMEM] *...  5.35 us
    pallas_call x1, Pallas kernels, form_beams(): pl.pallas_call(beam_kernel, in_specs=[IN_VMEM, IN_VMEM, IN_HBM, IN_HBM, I...  4.76 us
    ppermute x1, starting transfers between devices, from_behind(): return lax.ppermute(block, axis, route)  4.04 us
    pallas_call x1, Pallas kernels, one_hots(): pl.pallas_call(one_hot_kernel, in_specs=[IN_VMEM] * 3, out_specs=[IN_VMEM...  3.24 us
    pallas_call x1, Pallas kernels, channelize_first(): pl.pallas_call(first_kernel, in_specs=[IN_VMEM] * 6, out_specs=IN_HBM, ou...  2.13 us
  transfers between devices with their start and end apart: 2, of which 1 were waited for; matrix products, arithmetic and copies ran while one was open for 0% of the time, Pallas kernels for 11%

profile of v5, /device:TPU:1, one launch (start us, length us, event | category | flops | bytes accessed | tf_op | source)
XLA Modules:
  0.0 80.1 jit_solution(16982941729301972201)
XLA Ops:
  0.0 0.9 %slice.3 = bf16[16,6144]{1,0:T(8,128)(2,1)S(1)} slice(bf16[16,32768]{1,0:T(8,128)(2,1)} %x_hbm.1), slice={[0:16], [26624:32768]} | slice | bytes 393216 | tf_op jit(solution)/shard_map/slice | solution.py:504
  0.9 4.0 %collective-permute-start = (bf16[16,6144]{1,0:T(8,128)(2,1)S(1)}, bf16[16,6144]{1,0:T(8,128)(2,1)S(1)}, u32[]{:S(2)}, u32[]{:S(2)}) collective-permute-start(bf16[16,6144]{1,0:T(8,128)(2,1)S(1)} %slice.3), channel_id=1, source_target_pairs={{0,1},{2,3},{4,5},{6,7},{8,9},{10,11},{12,13},{14,15},{16,17},{18,... | collective-permute-start | bytes 589832 | tf_op jit(solution)/shard_map/ppermute | solution.py:38
  5.0 5.4 %channelize_later.1 = (bf16[16,32768]{1,0:T(8,128)(2,1)S(1)}, f32[4,2048]{1,0:T(4,128)S(1)}, bf16[4,2,1024,256]{3,2,1,0:T(8,128)(2,1)S(1)}, bf16[2048,256]{1,0:T(8,128)(2,1)S(1)}, f32[4,32,256]{2,1,0:T(8,128)S(1)}) custom-call(bf16[16,32768]{1,0:T(8,128)(2,1)} %x_hbm.1, f32[4,2048]{1,0:T(4,128)} %constant.12.clone.w_hbm, ...), custom_call_target="tpu_custom_call" | custom-call | flops 1073741824 | bytes 7340032 | tf_op jit(solution)/shard_map/channelize_later/pallas_call | solution.py:247
  10.4 0.0 collective-permute-done.prior_ref
  10.4 0.0 copy-start
  10.4 0.0 copy-start.1
  10.4 0.0 copy-start.4
  10.4 0.0 copy-start.2
  10.4 0.0 copy-start.3
  10.4 2.1 %channelize_first.1 = bf16[2048,256]{1,0:T(8,128)(2,1)} custom-call(bf16[16,32768]{1,0:T(8,128)(2,1)S(1)} %get-tuple-element.13.x_ref, bf16[16,6144]{1,0:T(8,128)(2,1)S(1)} %collective-permute-done.prior_ref, f32[4,2048]{1,0:T(4,128)S(1)} %get-tuple-element.14.w_ref, bf16[4,2,1024,256]{3,2,1,0:T(8,128)(2,1)S(1)} %get-tuple-element.15.t_ref, ...), custom_call_target="tpu_custom_call" | custom-call | flops 201326592 | bytes 7340032 | tf_op jit(solution)/shard_map/channelize_first/pallas_call | solution.py:284
  12.6 16.8 %all-to-all-start = ((bf16[128,16,256]{2,1,0:T(8,128)(2,1)}), bf16[128,16,256]{2,1,0:T(8,128)(2,1)S(1)}, u32[]{:S(2)}, u32[]{:S(2)}) async-start(bf16[128,16,256]{2,1,0:T(8,128)(2,1)} %bitcast), calls=%async_computation | async-start | bytes 2097152 | tf_op jit(solution)/shard_map/all_to_all | solution.py:42
  29.4 0.0 copy-done
  29.4 0.0 copy-done.1
  29.4 0.0 copy-done.4
  29.4 3.2 %one_hots.1 = (bf16[256,2048]{1,0:T(8,128)(2,1)S(1)}, bf16[1024,2048]{1,0:T(8,128)(2,1)}, bf16[1024,1024]{1,0:T(8,128)(2,1)}) custom-call(s32[16,128]{1,0:T(8,128)S(1)} %bitcast.7, s32[8,128]{1,0:T(8,128)S(1)} %bitcast.9, s32[1,2048]{1,0:T(1,128)S(1)} %copy-done.4), custom_call_target="tpu_custom_call" | custom-call | flops 20971520 | bytes 10485760 | tf_op jit(solution)/shard_map/one_hots/pallas_call | solution.py:335
  32.7 19.8 %all-to-all-done = bf16[128,16,256]{2,1,0:T(8,128)(2,1)S(1)} async-done(((bf16[128,16,256]{2,1,0:T(8,128)(2,1)}), bf16[128,16,256]{2,1,0:T(8,128)(2,1)S(1)}, u32[]{:S(2)}, u32[]{:S(2)}) %all-to-all-start) | async-done | bytes 1048608 | tf_op jit(solution)/shard_map/all_to_all | solution.py:42
  52.5 0.0 copy-done.2
  52.5 0.0 copy-done.3
  52.5 4.8 %form_beams.1 = bf16[1024,128]{1,0:T(8,128)(2,1)S(1)} custom-call(bf16[2048,256]{1,0:T(8,128)(2,1)S(1)} %bitcast.5, bf16[256,2048]{1,0:T(8,128)(2,1)S(1)} %get-tuple-element.18.head_ref, bf16[1024,2048]{1,0:T(8,128)(2,1)} %get-tuple-element.19.rest_hbm, bf16[1024,1024]{1,0:T(8,128)(2,1)} %get-tuple-element.20.turn_hbm, bf16[512,256]{1,0:T(8,128)(2,1)S(1)} %copy-done.2, ...), custom_call_target="tpu_custom_call" | custom-call | flops 3145728000 | bytes 12582912 | tf_op jit(solution)/shard_map/form_beams/pallas_call | solution.py:455
  57.3 22.0 %all_to_all.20.x_ref = bf16[128,8,128]{2,1,0:T(8,128)(2,1)S(1)} all-to-all(bf16[128,8,128]{2,1,0:T(8,128)(2,1)S(1)} %bitcast.6), channel_id=1, replica_groups={{254,252,250,248,222,220,218,216,246,244,242,240,214,212,210,208,238,23..., dimensions={0} | all-to-all | bytes 524288 | tf_op jit(solution)/shard_map/all_to_all | solution.py:42
  79.3 0.8 %widen.1 = f32[1,8,16384]{2,1,0:T(8,128)} custom-call(bf16[128,8,128]{2,1,0:T(8,128)(2,1)S(1)} %all_to_all.20.x_ref), custom_call_target="tpu_custom_call" | custom-call | tf_op jit(solution)/shard_map/widen/pallas_call | solution.py:495
Async XLA Ops:
  0.9 9.4 %collective-permute-start = (bf16[16,6144]{1,0:T(8,128)(2,1)S(1)}, bf16[16,6144]{1,0:T(8,128)(2,1)S(1)}, u32[]{:S(2)}, u32[]{:S(2)}) collective-permute-start(bf16[16,6144]{1,0:T(8,128)(2,1)S(1)} %slice.3), channel_id=1, source_target_pairs={{0,1},{2,3},{4,5},{6,7},{8,9},{10,11},{12,13},{14,15},{16,17},{18,... | collective-permute-start | bytes 589832 | tf_op jit(solution)/shard_map/ppermute | solution.py:38
  10.4 19.1 %copy-start = (s32[2048]{0:T(1024)S(1)}, s32[2048]{0:T(1024)}, u32[]{:S(2)}) copy-start(s32[2048]{0:T(1024)} %param.12) | copy-start | bytes 24580
  10.4 19.1 %copy-start.1 = (s32[1024]{0:T(1024)S(1)}, s32[1024]{0:T(1024)}, u32[]{:S(2)}) copy-start(s32[1024]{0:T(1024)} %param.13) | copy-start | bytes 12292
  10.4 19.1 %copy-start.4 = (s32[1,2048]{1,0:T(1,128)S(1)}, s32[1,2048]{1,0:T(1,128)}, u32[]{:S(2)}) copy-start(s32[1,2048]{1,0:T(1,128)} %constant.15.clone.ids_ref) | copy-start | bytes 24580
  10.4 42.1 %copy-start.2 = (bf16[512,256]{1,0:T(8,128)(2,1)S(1)}, bf16[512,256]{1,0:T(8,128)(2,1)}, u32[]{:S(2)}) copy-start(bf16[512,256]{1,0:T(8,128)(2,1)} %constant.16.clone.north_ref) | copy-start | bytes 786436
  10.4 42.1 %copy-start.3 = (bf16[256,256]{1,0:T(8,128)(2,1)S(1)}, bf16[256,256]{1,0:T(8,128)(2,1)}, u32[]{:S(2)}) copy-start(bf16[256,256]{1,0:T(8,128)(2,1)} %constant.17.clone.fine_ref) | copy-start | bytes 393220
  12.6 40.0 %all-to-all-start = ((bf16[128,16,256]{2,1,0:T(8,128)(2,1)}), bf16[128,16,256]{2,1,0:T(8,128)(2,1)S(1)}, u32[]{:S(2)}, u32[]{:S(2)}) async-start(bf16[128,16,256]{2,1,0:T(8,128)(2,1)} %bitcast), calls=%async_computation | async-start | bytes 2097152 | tf_op jit(solution)/shard_map/all_to_all | solution.py:42

commit v6 on v5

--- a/solution.py
+++ b/solution.py
@@ -29,7 +29,7 @@
 HEAD = 256
 ROWS = 64
 MADE = 1024
-RING = [x * 32 + z * 4 + k for x in (3, 2, 1, 0) for z in (7, 3, 6, 2, 5, 1, 4, 0) for k in (3, 2, 1, 0)]
+RING = [x * 32 + z * 4 + k for zs in ((7, 3), (6, 2), (5, 1), (4, 0)) for x in (3, 2, 1, 0) for z in zs for k in (3, 2, 1, 0)]
 
 
 def from_behind(block, axis, distance):

time: 80.4 us -> 80.1 us (level)
  blocking collectives: 22 us -> 20.9 us
    all_to_all x1, blocking collectives: 22 us -> 20.9 us  [exchange(): lax.all_to_all(block, 'gx', split_axis=0, concat_axis=0, axis_index_group...]
    all_to_all x1, waiting for transfers between devices: 19.8 us -> 20.6 us  [exchange(): lax.all_to_all(block, 'gx', split_axis=0, concat_axis=0, axis_index_group...]
where the time goes in v6:
time: 80.1 us; the launch traced here: 79.8 us
  starting transfers between devices  20.9 us (26%)
  blocking collectives  20.9 us (26%)
  waiting for transfers between devices  20.6 us (26%)
  Pallas kernels  16.3 us (20%)
  local copies, waits for them, and re-layouts  0.97 us (1%)
    all_to_all x1, blocking collectives, exchange(): lax.all_to_all(block, 'gx', split_axis=0, concat_axis=0, axis_index_group...  20.9 us
    all_to_all x1, waiting for transfers between devices, exchange(): lax.all_to_all(block, 'gx', split_axis=0, concat_axis=0, axis_index_group...  20.6 us
    all_to_all x1, starting transfers between devices, exchange(): lax.all_to_all(block, 'gx', split_axis=0, concat_axis=0, axis_index_group...  16.8 us
    pallas_call x1, Pallas kernels, channelize_later(): pl.pallas_call(later_kernel, in_specs=[IN_HBM] * 5, out_specs=[IN_VMEM] *...  5.35 us
    pallas_call x1, Pallas kernels, form_beams(): pl.pallas_call(beam_kernel, in_specs=[IN_VMEM, IN_VMEM, IN_HBM, IN_HBM, I...  4.76 us
    ppermute x1, starting transfers between devices, from_behind(): return lax.ppermute(block, axis, route)  4.04 us
    pallas_call x1, Pallas kernels, one_hots(): pl.pallas_call(one_hot_kernel, in_specs=[IN_VMEM] * 3, out_specs=[IN_VMEM...  3.24 us
    pallas_call x1, Pallas kernels, channelize_first(): pl.pallas_call(first_kernel, in_specs=[IN_VMEM] * 6, out_specs=IN_HBM, ou...  2.13 us
  transfers between devices with their start and end apart: 2, of which 1 were waited for; matrix products, arithmetic and copies ran while one was open for 0% of the time, Pallas kernels for 11%

profile of v6, /device:TPU:1, one launch (start us, length us, event | category | flops | bytes accessed | tf_op | source)
XLA Modules:
  0.0 79.8 jit_solution(13487852619209679696)
XLA Ops:
  0.0 0.9 %slice.3 = bf16[16,6144]{1,0:T(8,128)(2,1)S(1)} slice(bf16[16,32768]{1,0:T(8,128)(2,1)} %x_hbm.1), slice={[0:16], [26624:32768]} | slice | bytes 393216 | tf_op jit(solution)/shard_map/slice | solution.py:504
  0.9 4.0 %collective-permute-start = (bf16[16,6144]{1,0:T(8,128)(2,1)S(1)}, bf16[16,6144]{1,0:T(8,128)(2,1)S(1)}, u32[]{:S(2)}, u32[]{:S(2)}) collective-permute-start(bf16[16,6144]{1,0:T(8,128)(2,1)S(1)} %slice.3), channel_id=1, source_target_pairs={{0,1},{2,3},{4,5},{6,7},{8,9},{10,11},{12,13},{14,15},{16,17},{18,... | collective-permute-start | bytes 589832 | tf_op jit(solution)/shard_map/ppermute | solution.py:38
  5.0 5.4 %channelize_later.1 = (bf16[16,32768]{1,0:T(8,128)(2,1)S(1)}, f32[4,2048]{1,0:T(4,128)S(1)}, bf16[4,2,1024,256]{3,2,1,0:T(8,128)(2,1)S(1)}, bf16[2048,256]{1,0:T(8,128)(2,1)S(1)}, f32[4,32,256]{2,1,0:T(8,128)S(1)}) custom-call(bf16[16,32768]{1,0:T(8,128)(2,1)} %x_hbm.1, f32[4,2048]{1,0:T(4,128)} %constant.12.clone.w_hbm, ...), custom_call_target="tpu_custom_call" | custom-call | flops 1073741824 | bytes 7340032 | tf_op jit(solution)/shard_map/channelize_later/pallas_call | solution.py:247
  10.4 0.0 collective-permute-done.prior_ref
  10.4 0.0 copy-start
  10.4 0.0 copy-start.1
  10.4 0.0 copy-start.4
  10.4 0.0 copy-start.2
  10.4 0.0 copy-start.3
  10.4 2.1 %channelize_first.1 = bf16[2048,256]{1,0:T(8,128)(2,1)} custom-call(bf16[16,32768]{1,0:T(8,128)(2,1)S(1)} %get-tuple-element.13.x_ref, bf16[16,6144]{1,0:T(8,128)(2,1)S(1)} %collective-permute-done.prior_ref, f32[4,2048]{1,0:T(4,128)S(1)} %get-tuple-element.14.w_ref, bf16[4,2,1024,256]{3,2,1,0:T(8,128)(2,1)S(1)} %get-tuple-element.15.t_ref, ...), custom_call_target="tpu_custom_call" | custom-call | flops 201326592 | bytes 7340032 | tf_op jit(solution)/shard_map/channelize_first/pallas_call | solution.py:284
  12.6 16.8 %all-to-all-start = ((bf16[128,16,256]{2,1,0:T(8,128)(2,1)}), bf16[128,16,256]{2,1,0:T(8,128)(2,1)S(1)}, u32[]{:S(2)}, u32[]{:S(2)}) async-start(bf16[128,16,256]{2,1,0:T(8,128)(2,1)} %bitcast), calls=%async_computation | async-start | bytes 2097152 | tf_op jit(solution)/shard_map/all_to_all | solution.py:42
  29.4 0.0 copy-done
  29.4 0.0 copy-done.1
  29.4 0.0 copy-done.4
  29.4 3.2 %one_hots.1 = (bf16[256,2048]{1,0:T(8,128)(2,1)S(1)}, bf16[1024,2048]{1,0:T(8,128)(2,1)}, bf16[1024,1024]{1,0:T(8,128)(2,1)}) custom-call(s32[16,128]{1,0:T(8,128)S(1)} %bitcast.7, s32[8,128]{1,0:T(8,128)S(1)} %bitcast.9, s32[1,2048]{1,0:T(1,128)S(1)} %copy-done.4), custom_call_target="tpu_custom_call" | custom-call | flops 20971520 | bytes 10485760 | tf_op jit(solution)/shard_map/one_hots/pallas_call | solution.py:335
  32.7 20.6 %all-to-all-done = bf16[128,16,256]{2,1,0:T(8,128)(2,1)S(1)} async-done(((bf16[128,16,256]{2,1,0:T(8,128)(2,1)}), bf16[128,16,256]{2,1,0:T(8,128)(2,1)S(1)}, u32[]{:S(2)}, u32[]{:S(2)}) %all-to-all-start) | async-done | bytes 1048608 | tf_op jit(solution)/shard_map/all_to_all | solution.py:42
  53.3 0.0 copy-done.2
  53.3 0.0 copy-done.3
  53.3 4.8 %form_beams.1 = bf16[1024,128]{1,0:T(8,128)(2,1)S(1)} custom-call(bf16[2048,256]{1,0:T(8,128)(2,1)S(1)} %bitcast.5, bf16[256,2048]{1,0:T(8,128)(2,1)S(1)} %get-tuple-element.18.head_ref, bf16[1024,2048]{1,0:T(8,128)(2,1)} %get-tuple-element.19.rest_hbm, bf16[1024,1024]{1,0:T(8,128)(2,1)} %get-tuple-element.20.turn_hbm, bf16[512,256]{1,0:T(8,128)(2,1)S(1)} %copy-done.2, ...), custom_call_target="tpu_custom_call" | custom-call | flops 3145728000 | bytes 12582912 | tf_op jit(solution)/shard_map/form_beams/pallas_call | solution.py:455
  58.1 20.9 %all_to_all.20.x_ref = bf16[128,8,128]{2,1,0:T(8,128)(2,1)S(1)} all-to-all(bf16[128,8,128]{2,1,0:T(8,128)(2,1)S(1)} %bitcast.6), channel_id=1, replica_groups={{254,252,250,248,222,220,218,216,190,188,186,184,158,156,154,152,126,12..., dimensions={0} | all-to-all | bytes 524288 | tf_op jit(solution)/shard_map/all_to_all | solution.py:42
  79.0 0.8 %widen.1 = f32[1,8,16384]{2,1,0:T(8,128)} custom-call(bf16[128,8,128]{2,1,0:T(8,128)(2,1)S(1)} %all_to_all.20.x_ref), custom_call_target="tpu_custom_call" | custom-call | tf_op jit(solution)/shard_map/widen/pallas_call | solution.py:495
Async XLA Ops:
  0.9 9.4 %collective-permute-start = (bf16[16,6144]{1,0:T(8,128)(2,1)S(1)}, bf16[16,6144]{1,0:T(8,128)(2,1)S(1)}, u32[]{:S(2)}, u32[]{:S(2)}) collective-permute-start(bf16[16,6144]{1,0:T(8,128)(2,1)S(1)} %slice.3), channel_id=1, source_target_pairs={{0,1},{2,3},{4,5},{6,7},{8,9},{10,11},{12,13},{14,15},{16,17},{18,... | collective-permute-start | bytes 589832 | tf_op jit(solution)/shard_map/ppermute | solution.py:38
  10.4 19.1 %copy-start = (s32[2048]{0:T(1024)S(1)}, s32[2048]{0:T(1024)}, u32[]{:S(2)}) copy-start(s32[2048]{0:T(1024)} %param.12) | copy-start | bytes 24580
  10.4 19.1 %copy-start.1 = (s32[1024]{0:T(1024)S(1)}, s32[1024]{0:T(1024)}, u32[]{:S(2)}) copy-start(s32[1024]{0:T(1024)} %param.13) | copy-start | bytes 12292
  10.4 19.1 %copy-start.4 = (s32[1,2048]{1,0:T(1,128)S(1)}, s32[1,2048]{1,0:T(1,128)}, u32[]{:S(2)}) copy-start(s32[1,2048]{1,0:T(1,128)} %constant.15.clone.ids_ref) | copy-start | bytes 24580
  10.4 42.9 %copy-start.2 = (bf16[512,256]{1,0:T(8,128)(2,1)S(1)}, bf16[512,256]{1,0:T(8,128)(2,1)}, u32[]{:S(2)}) copy-start(bf16[512,256]{1,0:T(8,128)(2,1)} %constant.16.clone.north_ref) | copy-start | bytes 786436
  10.4 42.9 %copy-start.3 = (bf16[256,256]{1,0:T(8,128)(2,1)S(1)}, bf16[256,256]{1,0:T(8,128)(2,1)}, u32[]{:S(2)}) copy-start(bf16[256,256]{1,0:T(8,128)(2,1)} %constant.17.clone.fine_ref) | copy-start | bytes 393220
  12.6 40.8 %all-to-all-start = ((bf16[128,16,256]{2,1,0:T(8,128)(2,1)}), bf16[128,16,256]{2,1,0:T(8,128)(2,1)S(1)}, u32[]{:S(2)}, u32[]{:S(2)}) async-start(bf16[128,16,256]{2,1,0:T(8,128)(2,1)} %bitcast), calls=%async_computation | async-start | bytes 2097152 | tf_op jit(solution)/shard_map/all_to_all | solution.py:42
